TPU v7x, 32 devices: a whole 2x2x4 slice. The times are simulated.
32 devices in a mesh: dp: 8 (over z, y), tensor: 4 (over x, core).
Axes of the slice: x: 2, y: 2, z: 4, core: 2. Of those that a mesh axis runs over, the one named last changes fastest.
Arguments:
- tokens: bfloat16 [4096, 768], P(('dp', 'tensor')), may hold values from -6 to 6
- crop_depth: int32 [8], P('dp'), may hold values from 4 to 8, as said below
- w_query: float32 [768, 768], P('dp', 'tensor'), may hold values from -0.21875 to 0.21875
- w_key: float32 [768, 768], P('dp', 'tensor'), may hold values from -0.21875 to 0.21875
- w_value: float32 [768, 768], P('dp', 'tensor'), may hold values from -0.21875 to 0.21875
- w_out: float32 [768, 768], P('tensor', 'dp'), may hold values from -2.5 to 2.5
- w_up: float32 [768, 3072], P('dp', 'tensor'), may hold values from -0.21875 to 0.21875
- w_down: float32 [3072, 768], P('tensor', 'dp'), may hold values from -0.109375 to 0.109375
- w_tconv: float32 [768, 1024], P('dp', 'tensor'), may hold values from -0.21875 to 0.21875
- w_conv1: float32 [128, 27, 128], P('dp', None, 'tensor'), may hold values from -0.109375 to 0.109375
- w_conv2: float32 [128, 27, 128], P('dp', None, 'tensor'), may hold values from -0.109375 to 0.109375
- ln1_gain: float32 [768], P('dp'), may hold values from 0.1 to 1.9
- ln1_bias: float32 [768], P('dp'), may hold values from -3 to 3
- ln2_gain: float32 [768], P('dp'), may hold values from 0.1 to 1.9
- ln2_bias: float32 [768], P('dp'), may hold values from -3 to 3
- cot_out: float32 [4096, 768], P(('dp', 'tensor')), may hold values from -6 to 6
- cot_dec: float32 [8, 16, 16, 16, 128], P('dp', None, None, None, 'tensor'), may hold values from -6 to 6
Outputs:
- out_rows: float32 [4096, 768], P(('dp', 'tensor'))
- dec_out: float32 [8, 16, 16, 16, 128], P('dp', None, None, None, 'tensor')
- grad_tokens: float32 [4096, 768], P(('dp', 'tensor'))
- grad_w_query: float32 [768, 768], P('dp', 'tensor')
- grad_w_key: float32 [768, 768], P('dp', 'tensor')
- grad_w_value: float32 [768, 768], P('dp', 'tensor')
- grad_w_out: float32 [768, 768], P('tensor', 'dp')
- grad_w_up: float32 [768, 3072], P('dp', 'tensor')
- grad_w_down: float32 [3072, 768], P('tensor', 'dp')
- grad_w_tconv: float32 [768, 1024], P('dp', 'tensor')
- grad_w_conv1: float32 [128, 27, 128], P('dp', None, 'tensor')
- grad_w_conv2: float32 [128, 27, 128], P('dp', None, 'tensor')
- grad_ln1_gain: float32 [768], P('dp')
- grad_ln1_bias: float32 [768], P('dp')
- grad_ln2_gain: float32 [768], P('dp')
- grad_ln2_bias: float32 [768], P('dp')
Inputs may be any that keep to these rules, and one draw needn't show every extreme that they name: `crop_depth`: every crop has at least half of its depth slices live, and in every draw some crop has all 8 live.
All inputs are finite; a program needn't handle non-finite values.
Results may differ from a plain program's by a relative error of at most 0.035.
Values may be sent and summed in bfloat16 or wider, within the bound.
No kernel may reach another device: no remote copies, remote signals or barrier semaphores. Data moves between devices by JAX's collectives and lax.ppermute only.
A program may use at most 320 MiB of HBM per device.

v0:
```python
import jax
import jax.numpy as jnp
from jax import lax
from jax.sharding import PartitionSpec as P

HD = 64
GRID = 8


def layer_norm(rows):
    middle = jnp.mean(rows, axis=-1, keepdims=True)
    centred = rows - middle
    spread = jnp.mean(centred * centred, axis=-1, keepdims=True)
    return centred * lax.rsqrt(spread + 1e-06)


def norm_affine(rows, gain, shift):
    return layer_norm(rows) * gain + shift


def gelu_exact(value):
    return jax.nn.gelu(value, approximate=False)


def norm_act(conv_out, vox_mask):
    live = jnp.sum(vox_mask, axis=1, keepdims=True) * conv_out.shape[2] * conv_out.shape[3]
    middle = jnp.sum(conv_out * vox_mask, axis=(1, 2, 3), keepdims=True) / live
    centred = (conv_out - middle) * vox_mask
    spread = jnp.sum(centred * centred, axis=(1, 2, 3), keepdims=True) / live
    normed = (conv_out - middle) * lax.rsqrt(spread + 1e-05)
    return gelu_exact(normed) * vox_mask


def gather_rows(rows):
    return lax.all_gather(rows, "tensor", axis=0, tiled=True)


def scatter_rows(terms):
    return lax.psum_scatter(
        terms.astype(jnp.bfloat16), "tensor", scatter_dimension=0, tiled=True
    ).astype(jnp.float32)


def gather_channels(field):
    return lax.all_gather(field, "tensor", axis=4, tiled=True)


def scatter_channels(terms):
    return lax.psum_scatter(
        terms.astype(jnp.bfloat16), "tensor", scatter_dimension=4, tiled=True
    ).astype(jnp.float32)


def fetch_weights(
    w_query,
    w_key,
    w_value,
    w_out,
    w_up,
    w_down,
    w_tconv,
    w_conv1,
    w_conv2,
    ln1_gain,
    ln1_bias,
    ln2_gain,
    ln2_bias,
):
    low_type = jnp.bfloat16
    return (
        lax.all_gather(w_query.astype(low_type), "dp", axis=0, tiled=True),
        lax.all_gather(w_key.astype(low_type), "dp", axis=0, tiled=True),
        lax.all_gather(w_value.astype(low_type), "dp", axis=0, tiled=True),
        lax.all_gather(w_out.astype(low_type), "dp", axis=1, tiled=True),
        lax.all_gather(w_up.astype(low_type), "dp", axis=0, tiled=True),
        lax.all_gather(w_down.astype(low_type), "dp", axis=1, tiled=True),
        lax.all_gather(w_tconv.astype(low_type), "dp", axis=0, tiled=True),
        lax.all_gather(w_conv1.astype(low_type), "dp", axis=0, tiled=True),
        lax.all_gather(w_conv2.astype(low_type), "dp", axis=0, tiled=True),
        lax.all_gather(ln1_gain.astype(low_type), "dp", axis=0, tiled=True),
        lax.all_gather(ln1_bias.astype(low_type), "dp", axis=0, tiled=True),
        lax.all_gather(ln2_gain.astype(low_type), "dp", axis=0, tiled=True),
        lax.all_gather(ln2_bias.astype(low_type), "dp", axis=0, tiled=True),
    )


def refetch_weights(w_query, w_key, w_value, w_out, w_up, w_down, w_tconv, w_conv1, w_conv2):
    low_type = jnp.bfloat16
    return (
        lax.all_gather(w_query.astype(low_type), "dp", axis=0, tiled=True),
        lax.all_gather(w_key.astype(low_type), "dp", axis=0, tiled=True),
        lax.all_gather(w_value.astype(low_type), "dp", axis=0, tiled=True),
        lax.all_gather(w_out.astype(low_type), "dp", axis=1, tiled=True),
        lax.all_gather(w_up.astype(low_type), "dp", axis=0, tiled=True),
        lax.all_gather(w_down.astype(low_type), "dp", axis=1, tiled=True),
        lax.all_gather(w_tconv.astype(low_type), "dp", axis=0, tiled=True),
        lax.all_gather(w_conv1.astype(low_type), "dp", axis=0, tiled=True),
        lax.all_gather(w_conv2.astype(low_type), "dp", axis=0, tiled=True),
    )


def contract_first(left, right):
    return lax.dot_general(
        left, right, (((0,), (0,)), ((), ())), preferred_element_type=jnp.float32
    )


def contract_last(left, right):
    return lax.dot_general(
        left, right, (((1,), (1,)), ((), ())), preferred_element_type=jnp.float32
    )


def pad_cube(field):
    return jnp.pad(field, ((0, 0), (1, 1), (1, 1), (1, 1), (0, 0)))


def shifted(padded, offset, vox):
    deep, tall, wide = (offset // 9, offset // 3 % 3, offset % 3)
    block = padded[:, deep : deep + vox, tall : tall + vox, wide : wide + vox, :]
    return block.reshape(-1, block.shape[-1])


def conv_forward(field, kernel):
    vox = field.shape[1]
    chan_out = kernel.shape[2]
    padded = pad_cube(field)
    wide_kernel = kernel.reshape(kernel.shape[0], 27 * chan_out)
    products = jnp.dot(
        padded.reshape(-1, padded.shape[-1]), wide_kernel, preferred_element_type=jnp.float32
    )
    products = products.reshape(padded.shape[:4] + (27, chan_out))
    summed = jnp.zeros(field.shape[:4] + (chan_out,), jnp.float32)
    for offset in range(27):
        deep, tall, wide = (offset // 9, offset // 3 % 3, offset % 3)
        summed = (
            summed + products[:, deep : deep + vox, tall : tall + vox, wide : wide + vox, offset, :]
        )
    return summed


def grad_columns(grad_out):
    vox = grad_out.shape[1]
    padded = pad_cube(grad_out)
    return jnp.concatenate([shifted(padded, 26 - offset, vox) for offset in range(27)], axis=1)


def conv_input_grad(columns, kernel, shape_out):
    chan_in = kernel.shape[0]
    stacked = kernel.transpose(1, 2, 0).reshape(27 * kernel.shape[2], chan_in)
    summed = jnp.dot(columns, stacked, preferred_element_type=jnp.float32)
    return summed.reshape(shape_out[:4] + (chan_in,))


def conv_weight_grad(field, columns):
    flat_field = field.reshape(-1, field.shape[-1])
    product = contract_first(flat_field, columns)
    return product.reshape(field.shape[-1], 27, columns.shape[1] // 27)


def to_grid(rows, crops, grid, chans):
    cube = rows.reshape(crops, grid, grid, grid, chans, 2, 2, 2)
    cube = cube.transpose(0, 1, 5, 2, 6, 3, 7, 4)
    return cube.reshape(crops, 2 * grid, 2 * grid, 2 * grid, chans)


def from_grid(field, crops, grid, chans):
    cube = field.reshape(crops, grid, 2, grid, 2, grid, 2, chans)
    cube = cube.transpose(0, 1, 3, 5, 7, 2, 4, 6)
    return cube.reshape(crops * grid**3, chans * 8)


def shards(
    tokens,
    crop_depth,
    w_query,
    w_key,
    w_value,
    w_out,
    w_up,
    w_down,
    w_tconv,
    w_conv1,
    w_conv2,
    ln1_gain,
    ln1_bias,
    ln2_gain,
    ln2_bias,
    cot_out,
    cot_dec,
):
    low_type = jnp.bfloat16
    crops = crop_depth.shape[0]
    grid = GRID
    vox = 2 * grid
    patches = grid**3
    factor = HD ** (-0.5)
    fetched = fetch_weights(
        w_query,
        w_key,
        w_value,
        w_out,
        w_up,
        w_down,
        w_tconv,
        w_conv1,
        w_conv2,
        ln1_gain,
        ln1_bias,
        ln2_gain,
        ln2_bias,
    )
    (
        query_weight,
        key_weight,
        value_weight,
        out_weight,
        up_weight,
        down_weight,
        tconv_weight,
        conv1_weight,
        conv2_weight,
    ) = fetched[:9]
    gain_one = fetched[9].astype(jnp.float32)
    shift_one = fetched[10].astype(jnp.float32)
    gain_two = fetched[11].astype(jnp.float32)
    shift_two = fetched[12].astype(jnp.float32)
    heads_here = query_weight.shape[1] // HD

    def heads_view(flat):
        return flat.reshape(crops, patches, heads_here, HD)

    key_live = jnp.arange(patches)[None, :] // (grid * grid) < crop_depth[:, None]
    vox_mask = (jnp.arange(vox)[None, :] < 2 * crop_depth[:, None]).astype(jnp.float32)[
        :, :, None, None, None
    ]

    def score_block(query_rows, key_rows):
        raw = (
            jnp.einsum(
                "cqhd,ckhd->chqk",
                heads_view(query_rows),
                heads_view(key_rows),
                preferred_element_type=jnp.float32,
            )
            * factor
        )
        return jnp.where(key_live[:, None, None, :], raw, -1000000000.0)

    rows_in = tokens.astype(jnp.float32)
    normed1 = gather_rows(norm_affine(rows_in, gain_one, shift_one).astype(low_type))
    query = jnp.dot(normed1, query_weight, preferred_element_type=jnp.float32).astype(low_type)
    keys = jnp.dot(normed1, key_weight, preferred_element_type=jnp.float32).astype(low_type)
    values = jnp.dot(normed1, value_weight, preferred_element_type=jnp.float32).astype(low_type)
    scores = score_block(query, keys)
    peak = jnp.max(scores, axis=-1, keepdims=True)
    expo = jnp.exp(scores - peak)
    weight_sum = jnp.sum(expo, axis=-1, keepdims=True)
    probs = expo / weight_sum
    logsum = peak + jnp.log(weight_sum)
    attended = jnp.einsum(
        "chqk,ckhd->cqhd",
        probs.astype(low_type),
        heads_view(values),
        preferred_element_type=jnp.float32,
    )
    attended = attended.reshape(crops * patches, heads_here * HD).astype(low_type)
    middle_rows = rows_in + scatter_rows(
        jnp.dot(attended, out_weight, preferred_element_type=jnp.float32)
    )
    normed2 = gather_rows(norm_affine(middle_rows, gain_two, shift_two).astype(low_type))
    upper = jnp.dot(normed2, up_weight, preferred_element_type=jnp.float32)
    hidden = gelu_exact(upper).astype(low_type)
    after = middle_rows + scatter_rows(
        jnp.dot(hidden, down_weight, preferred_element_type=jnp.float32)
    )
    dec_in = gather_rows(after.astype(low_type))
    tconv = jnp.dot(dec_in, tconv_weight, preferred_element_type=jnp.float32)
    chans = tconv.shape[1] // 8
    first = gather_channels((to_grid(tconv, crops, grid, chans) * vox_mask).astype(low_type))
    conv_one = conv_forward(first, conv1_weight)
    act_one, act_one_back = jax.vjp(lambda value: norm_act(value, vox_mask), conv_one)
    act_full = gather_channels(act_one.astype(low_type))
    conv_two = conv_forward(act_full, conv2_weight)
    dec_out, act_two_back = jax.vjp(lambda value: norm_act(value, vox_mask), conv_two)
    refetched = refetch_weights(
        w_query, w_key, w_value, w_out, w_up, w_down, w_tconv, w_conv1, w_conv2
    )
    (
        query_weight,
        key_weight,
        value_weight,
        out_weight,
        up_weight,
        down_weight,
        tconv_weight,
        conv1_weight,
        conv2_weight,
    ) = refetched
    grad_conv_two = act_two_back(cot_dec)[0].astype(low_type)
    columns_two = grad_columns(grad_conv_two)
    wgrad_conv2 = conv_weight_grad(act_full, columns_two)
    grad_act_one = scatter_channels(conv_input_grad(columns_two, conv2_weight, act_full.shape))
    grad_conv_one = act_one_back(grad_act_one)[0].astype(low_type)
    columns_one = grad_columns(grad_conv_one)
    wgrad_conv1 = conv_weight_grad(first, columns_one)
    grad_first = scatter_channels(conv_input_grad(columns_one, conv1_weight, first.shape))
    grad_tconv = from_grid(grad_first * vox_mask, crops, grid, chans).astype(low_type)
    wgrad_tconv = contract_first(dec_in, grad_tconv)
    grad_after = cot_out + scatter_rows(contract_last(grad_tconv, tconv_weight))
    grad_mlp = gather_rows(grad_after.astype(low_type))
    wgrad_down = contract_first(hidden, grad_mlp)
    grad_hidden = contract_last(grad_mlp, down_weight)
    grad_upper = jax.vjp(gelu_exact, upper)[1](grad_hidden)[0].astype(low_type)
    wgrad_up = contract_first(normed2, grad_upper)
    grad_normed2 = scatter_rows(contract_last(grad_upper, up_weight))
    norm_two_back = jax.vjp(norm_affine, middle_rows, gain_two, shift_two)[1]
    grad_mid_norm, grad_gain_two, grad_shift_two = norm_two_back(grad_normed2)
    grad_middle = grad_after + grad_mid_norm
    grad_branch = gather_rows(grad_middle.astype(low_type))
    wgrad_out = contract_first(attended, grad_branch)
    grad_attended = contract_last(grad_branch, out_weight).astype(low_type)
    again_scores = score_block(query, keys)
    again_probs = jnp.exp(again_scores - logsum)
    grad_values = jnp.einsum(
        "chqk,cqhd->ckhd",
        again_probs.astype(low_type),
        heads_view(grad_attended),
        preferred_element_type=jnp.float32,
    )
    grad_probs = jnp.einsum(
        "cqhd,ckhd->chqk",
        heads_view(grad_attended),
        heads_view(values),
        preferred_element_type=jnp.float32,
    )
    inner = jnp.sum(again_probs * grad_probs, axis=-1, keepdims=True)
    grad_scores = (again_probs * (grad_probs - inner)).astype(low_type)
    grad_query = (
        jnp.einsum(
            "chqk,ckhd->cqhd", grad_scores, heads_view(keys), preferred_element_type=jnp.float32
        )
        * factor
    )
    grad_keys = (
        jnp.einsum(
            "chqk,cqhd->ckhd", grad_scores, heads_view(query), preferred_element_type=jnp.float32
        )
        * factor
    )
    width_here = heads_here * HD
    grad_query = grad_query.reshape(crops * patches, width_here).astype(low_type)
    grad_keys = grad_keys.reshape(crops * patches, width_here).astype(low_type)
    grad_values = grad_values.reshape(crops * patches, width_here).astype(low_type)
    wgrad_query = contract_first(normed1, grad_query)
    wgrad_key = contract_first(normed1, grad_keys)
    wgrad_value = contract_first(normed1, grad_values)
    grad_normed1 = scatter_rows(
        contract_last(grad_query, query_weight)
        + contract_last(grad_keys, key_weight)
        + contract_last(grad_values, value_weight)
    )
    norm_one_back = jax.vjp(norm_affine, rows_in, gain_one, shift_one)[1]
    grad_rows_norm, grad_gain_one, grad_shift_one = norm_one_back(grad_normed1)
    grad_tokens = grad_middle + grad_rows_norm
    gain_grads = lax.psum((grad_gain_one, grad_shift_one, grad_gain_two, grad_shift_two), "tensor")
    summed = (
        lax.psum_scatter(wgrad_query, "dp", scatter_dimension=0, tiled=True),
        lax.psum_scatter(wgrad_key, "dp", scatter_dimension=0, tiled=True),
        lax.psum_scatter(wgrad_value, "dp", scatter_dimension=0, tiled=True),
        lax.psum_scatter(wgrad_out, "dp", scatter_dimension=1, tiled=True),
        lax.psum_scatter(wgrad_up, "dp", scatter_dimension=0, tiled=True),
        lax.psum_scatter(wgrad_down, "dp", scatter_dimension=1, tiled=True),
        lax.psum_scatter(wgrad_tconv, "dp", scatter_dimension=0, tiled=True),
        lax.psum_scatter(wgrad_conv1, "dp", scatter_dimension=0, tiled=True),
        lax.psum_scatter(wgrad_conv2, "dp", scatter_dimension=0, tiled=True),
        lax.psum_scatter(gain_grads[0], "dp", scatter_dimension=0, tiled=True),
        lax.psum_scatter(gain_grads[1], "dp", scatter_dimension=0, tiled=True),
        lax.psum_scatter(gain_grads[2], "dp", scatter_dimension=0, tiled=True),
        lax.psum_scatter(gain_grads[3], "dp", scatter_dimension=0, tiled=True),
    )
    return (
        after,
        dec_out,
        grad_tokens,
        summed[0],
        summed[1],
        summed[2],
        summed[3],
        summed[4],
        summed[5],
        summed[6],
        summed[7],
        summed[8],
        summed[9],
        summed[10],
        summed[11],
        summed[12],
    )


def solution(mesh):
    in_specs = (
        P(("dp", "tensor"), None),
        P("dp"),
        P("dp", "tensor"),
        P("dp", "tensor"),
        P("dp", "tensor"),
        P("tensor", "dp"),
        P("dp", "tensor"),
        P("tensor", "dp"),
        P("dp", "tensor"),
        P("dp", None, "tensor"),
        P("dp", None, "tensor"),
        P("dp"),
        P("dp"),
        P("dp"),
        P("dp"),
        P(("dp", "tensor"), None),
        P("dp", None, None, None, "tensor"),
    )
    out_specs = (
        P(("dp", "tensor"), None),
        P("dp", None, None, None, "tensor"),
        P(("dp", "tensor"), None),
        P("dp", "tensor"),
        P("dp", "tensor"),
        P("dp", "tensor"),
        P("tensor", "dp"),
        P("dp", "tensor"),
        P("tensor", "dp"),
        P("dp", "tensor"),
        P("dp", None, "tensor"),
        P("dp", None, "tensor"),
        P("dp"),
        P("dp"),
        P("dp"),
        P("dp"),
    )
    return jax.shard_map(shards, mesh=mesh, in_specs=in_specs, out_specs=out_specs, check_vma=False)
```

profile of v0, /device:TPU:0, one launch (start us, length us, event | category | flops | bytes accessed | tf_op | source)
XLA Modules:
  0.0 1571.5 jit_solution(9408792050243969758)
XLA Ops:
  16.5 23.3 %all-reduce.14 = (bf16[768]{0:T(1024)(128)(2,1)S(1)}, bf16[768]{0:T(1024)(128)(2,1)S(1)}, bf16[768]{0:T(1024)(128)(2,1)S(1)}, bf16[768]{0:T(1024)(128)(2,1)S(1)}) all-reduce(bf16[768]{0:T(1024)(128)(2,1)S(1)} %dynamic-update-slice.1, bf16[768]{0:T(1024)(128)(2,1)S(1)} %dynamic-update-slice, ...), channel_id=1, replica_groups=mesh['dp'=8,'tensor'=4] {'dp'}, use_global_device_ids=true, to_apply=%add.5 | all-reduce | flops 3072 | bytes 12288
  43.6 31.0 %all_gather.75 = bf16[192,768]{0,1:T(8,128)(2,1)S(1)} all-gather(bf16[192,96]{0,1:T(8,128)(2,1)S(1)} %copy.156), channel_id=1, replica_groups=mesh['dp'=8,'tensor'=4] {'dp'}, dimensions={1}, use_global_device_ids=true | all-gather | bytes 331776 | tf_op jit(solution)/shard_map/all_gather | solution.py:74
  74.6 31.2 %all_gather.72 = bf16[768,192]{1,0:T(8,128)(2,1)S(1)} all-gather(bf16[96,192]{1,0:T(8,128)(2,1)S(1)} %convert_element_type.274), channel_id=1, replica_groups=mesh['dp'=8,'tensor'=4] {'dp'}, dimensions={0}, use_global_device_ids=true | all-gather | bytes 331776 | tf_op jit(solution)/shard_map/all_gather | solution.py:73
  105.8 30.9 %all_gather.74 = bf16[768,192]{1,0:T(8,128)(2,1)S(1)} all-gather(bf16[96,192]{1,0:T(8,128)(2,1)S(1)} %convert_element_type.278), channel_id=1, replica_groups=mesh['dp'=8,'tensor'=4] {'dp'}, dimensions={0}, use_global_device_ids=true | all-gather | bytes 331776 | tf_op jit(solution)/shard_map/all_gather | solution.py:72
  136.8 30.9 %all_gather.73 = bf16[768,192]{1,0:T(8,128)(2,1)S(1)} all-gather(bf16[96,192]{1,0:T(8,128)(2,1)S(1)} %convert_element_type.276), channel_id=1, replica_groups=mesh['dp'=8,'tensor'=4] {'dp'}, dimensions={0}, use_global_device_ids=true | all-gather | bytes 331776 | tf_op jit(solution)/shard_map/all_gather | solution.py:71
  183.9 18.2 %reduce-scatter.23.cloned.1.call-done = bf16[128,768]{1,0:T(8,128)(2,1)} async-done(((bf16[512,768]{1,0:T(8,128)(2,1)}), bf16[128,768]{1,0:T(8,128)(2,1)}) %reduce-scatter.23.cloned.1.call-update) | async-done | bytes 196624 | tf_op jit(solution)/shard_map/reduce_scatter | solution.py:39
  229.9 36.6 %all-gather.7.cloned.1.call-done = bf16[768,768]{0,1:T(8,128)(2,1)} async-done(((bf16[768,96]{0,1:T(8,128)(2,1)}), bf16[768,768]{0,1:T(8,128)(2,1)}) %all-gather.7.cloned.1.call-update) | async-done | bytes 1179664 | tf_op jit(solution)/shard_map/all_gather | solution.py:76
  269.7 31.0 %all_gather.82 = bf16[768,256]{1,0:T(8,128)(2,1)S(1)} all-gather(bf16[96,256]{1,0:T(8,128)(2,1)S(1)} %convert_element_type.299), channel_id=1, replica_groups=mesh['dp'=8,'tensor'=4] {'dp'}, dimensions={0}, use_global_device_ids=true | all-gather | bytes 442368 | tf_op jit(solution)/shard_map/all_gather | solution.py:77
  332.0 32.4 %all_gather.84 = bf16[128,27,32]{2,0,1:T(8,128)(2,1)S(1)} all-gather(bf16[16,27,32]{2,0,1:T(8,128)(2,1)S(1)} %convert_element_type.302), channel_id=1, replica_groups=mesh['dp'=8,'tensor'=4] {'dp'}, dimensions={0}, use_global_device_ids=true | all-gather | bytes 248832 | tf_op jit(solution)/shard_map/all_gather | solution.py:78
  365.3 22.2 %all-gather.9.cloned.1.call-done = bf16[1,16,16,16,128]{3,2,1,0,4:T(8,128)(2,1)} async-done(((bf16[1,16,16,16,32]{3,2,1,0,4:T(8,128)(2,1)}), bf16[1,16,16,16,128]{3,2,1,0,4:T(8,128)(2,1)}) %all-gather.9.cloned.1.call-update) | async-done | bytes 1048592 | tf_op jit(solution)/shard_map/all_gather | solution.py:45
  398.5 36.9 %convolution_bitcast_fusion.1 = f32[1,18,18,18,27,32]{5,3,4,2,1,0:T(8,128)} fusion(bf16[1,16,16,16,128]{4,3,2,1,0:T(8,128)(2,1)S(1)} %copy.160, bf16[128,27,32]{0,2,1:T(8,128)(2,1)S(1)} %copy.161), kind=kOutput, calls=%fused_computation.1 | convolution fusion | flops 1289945088 | bytes 21425152 | tf_op jit(solution)/shard_map/dot_general | solution.py:129
  435.4 25.0 %multiply_reduce_fusion.6 = (f32[32]{0:T(128)S(1)}, f32[1,16,16,16,32]{4,3,2,1,0:T(8,128)S(1)}) fusion(f32[16]{0:T(128)S(1)} %compare_convert_fusion.1, f32[1,18,18,18,27,32]{5,3,4,2,1,0:T(8,128)} %convolution_bitcast_fusion.1), kind=kLoop, calls=%fused_computation.196 | loop fusion | flops 3669984 | bytes 14680256 | tf_op jit(solution)/shard_map/jvp()/reduce_sum | solution.py:27
  471.0 32.8 %all_gather.86 = bf16[128,27,32]{2,0,1:T(8,128)(2,1)S(1)} all-gather(bf16[16,27,32]{2,0,1:T(8,128)(2,1)S(1)} %convert_element_type.305), channel_id=1, replica_groups=mesh['dp'=8,'tensor'=4] {'dp'}, dimensions={0}, use_global_device_ids=true | all-gather | bytes 248832 | tf_op jit(solution)/shard_map/all_gather | solution.py:79
  505.1 24.3 %all-gather.11.cloned.1.call-done = bf16[1,16,16,16,128]{3,2,1,0,4:T(8,128)(2,1)} async-done(((bf16[1,16,16,16,32]{3,2,1,0,4:T(8,128)(2,1)}), bf16[1,16,16,16,128]{3,2,1,0,4:T(8,128)(2,1)}) %all-gather.11.cloned.1.call-update) | async-done | bytes 1048592 | tf_op jit(solution)/shard_map/all_gather | solution.py:45
  539.4 37.0 %convolution_bitcast_fusion = f32[1,18,18,18,27,32]{5,3,2,1,4,0:T(8,128)} fusion(bf16[1,16,16,16,128]{4,3,2,1,0:T(8,128)(2,1)S(1)} %copy.189, bf16[128,27,32]{0,2,1:T(8,128)(2,1)S(1)} %copy.190), kind=kOutput, calls=%fused_computation | convolution fusion | flops 1289945088 | bytes 21425152 | tf_op jit(solution)/shard_map/dot_general | solution.py:129
  576.4 25.3 %multiply_reduce_fusion.4 = (f32[32]{0:T(128)S(1)}, f32[1,16,16,16,32]{4,3,2,1,0:T(8,128)S(1)}) fusion(f32[16]{0:T(128)S(1)} %compare_convert_fusion.1, f32[1,18,18,18,27,32]{5,3,2,1,4,0:T(8,128)} %convolution_bitcast_fusion), kind=kLoop, calls=%fused_computation.181 | loop fusion | flops 3669984 | bytes 14680256 | tf_op jit(solution)/shard_map/jvp()/reduce_sum | solution.py:27
  629.5 26.3 %concatenate.147 = bf16[16,16,16,864]{3,2,1,0:T(8,128)(2,1)} concatenate(bf16[16,16,16,32]{3,2,1,0:T(8,128)(2,1)} %get-tuple-element.86, bf16[16,16,16,32]{3,2,1,0:T(8,128)(2,1)} %get-tuple-element.85, bf16[16,16,16,32]{3,2,1,0:T(8,128)(2,1)} %get-tuple-element.84, bf16[16,16,16,32]{3,2,1,0:T(8,128)(2,1)} %get-tuple-element.83, bf16[16,16,16,32]{3,2,1,0:T(8,128)(2,1)} %get-tuple-element.82, ...), dimensions={3} | concatenate | bytes 14155776 | tf_op jit(solution)/shard_map/concatenate | solution.py:145
  689.2 24.7 %reduce-scatter.49.cloned.1.call-done = bf16[32,4096]{1,0:T(8,128)(2,1)} async-done(((bf16[128,4096]{1,0:T(8,128)(2,1)}), bf16[32,4096]{1,0:T(8,128)(2,1)}) %reduce-scatter.49.cloned.1.call-update) | async-done | bytes 262160
  742.7 26.0 %concatenate.175 = bf16[16,16,16,864]{3,2,1,0:T(8,128)(2,1)} concatenate(bf16[16,16,16,32]{3,2,1,0:T(8,128)(2,1)} %get-tuple-element.138, bf16[16,16,16,32]{3,2,1,0:T(8,128)(2,1)} %get-tuple-element.137, bf16[16,16,16,32]{3,2,1,0:T(8,128)(2,1)} %get-tuple-element.136, bf16[16,16,16,32]{3,2,1,0:T(8,128)(2,1)} %get-tuple-element.135, bf16[16,16,16,32]{3,2,1,0:T(8,128)(2,1)} %get-tuple-element.134, ...), dimensions={3} | concatenate | bytes 14155776 | tf_op jit(solution)/shard_map/concatenate | solution.py:145
  801.8 25.0 %reduce-scatter.51.cloned.1.call-done = bf16[32,4096]{1,0:T(8,128)(2,1)} async-done(((bf16[128,4096]{1,0:T(8,128)(2,1)}), bf16[32,4096]{1,0:T(8,128)(2,1)}) %reduce-scatter.51.cloned.1.call-update) | async-done | bytes 262160
  848.0 23.4 %reduce-scatter.27.cloned.1.call-done = bf16[128,768]{1,0:T(8,128)(2,1)} async-done(((bf16[512,768]{1,0:T(8,128)(2,1)}), bf16[128,768]{1,0:T(8,128)(2,1)}) %reduce-scatter.27.cloned.1.call-update) | async-done | bytes 196624 | tf_op jit(solution)/shard_map/reduce_scatter | solution.py:39
  886.1 23.7 %reduce-scatter.29.cloned.1.call-done = bf16[128,768]{1,0:T(8,128)(2,1)} async-done(((bf16[512,768]{1,0:T(8,128)(2,1)}), bf16[128,768]{1,0:T(8,128)(2,1)}) %reduce-scatter.29.cloned.1.call-update) | async-done | bytes 196624 | tf_op jit(solution)/shard_map/reduce_scatter | solution.py:39
  942.9 26.0 %concatenate.177 = bf16[4096,864]{1,0:T(8,128)(2,1)} concatenate(bf16[4096,32]{1,0:T(8,128)(2,1)} %bitcast.672, bf16[4096,32]{1,0:T(8,128)(2,1)S(1)} %bitcast.635, bf16[4096,32]{1,0:T(8,128)(2,1)} %bitcast.636, bf16[4096,32]{1,0:T(8,128)(2,1)} %bitcast.637, bf16[4096,32]{1,0:T(8,128)(2,1)} %bitcast.638, bf16[4096,32]{1,0:T(8,128)(2,1)} %bitcast.639, bf16[4096,32]{1,0:T(8,128)(2,1)} %bitcast.640, ...), dimensions={1} | concatenate | bytes 14155776 | tf_op jit(solution)/shard_map/concatenate | solution.py:145
  996.7 26.1 %concatenate.176 = bf16[4096,864]{1,0:T(8,128)(2,1)} concatenate(bf16[4096,32]{1,0:T(8,128)(2,1)} %bitcast.686, bf16[4096,32]{1,0:T(8,128)(2,1)S(1)} %bitcast.647, bf16[4096,32]{1,0:T(8,128)(2,1)} %bitcast.648, bf16[4096,32]{1,0:T(8,128)(2,1)} %bitcast.649, bf16[4096,32]{1,0:T(8,128)(2,1)} %bitcast.650, bf16[4096,32]{1,0:T(8,128)(2,1)} %bitcast.651, bf16[4096,32]{1,0:T(8,128)(2,1)} %bitcast.652, ...), dimensions={1} | concatenate | bytes 14155776 | tf_op jit(solution)/shard_map/concatenate | solution.py:145
  1060.2 37.3 %all-reduce.12 = (f32[768]{0:T(1024)S(1)}, f32[768]{0:T(1024)S(1)}, f32[768]{0:T(1024)S(1)}, f32[768]{0:T(1024)S(1)}) all-reduce(f32[768]{0:T(1024)S(1)} %get-tuple-element.22, f32[768]{0:T(1024)S(1)} %get-tuple-element.26, f32[768]{0:T(1024)S(1)} %copy-done.80, f32[768]{0:T(1024)S(1)} %copy-done.79), channel_id=18, replica_groups=mesh['dp'=8,'tensor'=4] {'dp'}, use_global_device_ids=true, to_apply=%region_40.41.clone | all-reduce | flops 3072 | bytes 24576
  1106.4 51.0 %reduce-scatter.45.cloned.1.call-done = f32[16,27,32]{2,0,1:T(8,128)} async-done(((f32[128,27,32]{2,0,1:T(8,128)}), f32[16,27,32]{2,0,1:T(8,128)}) %reduce-scatter.45.cloned.1.call-update) | async-done | bytes 55312 | tf_op jit(solution)/shard_map/reduce_scatter | solution.py:375
  1157.4 65.2 %reduce-scatter.43.cloned.1.call-done = f32[96,256]{1,0:T(8,128)} async-done(((f32[768,256]{1,0:T(8,128)}), f32[96,256]{1,0:T(8,128)}) %reduce-scatter.43.cloned.1.call-update) | async-done | bytes 98320 | tf_op jit(solution)/shard_map/reduce_scatter | solution.py:374
  1222.6 65.7 %reduce-scatter.37.cloned.1.call-done = f32[96,192]{1,0:T(8,128)} async-done(((f32[768,192]{1,0:T(8,128)}), f32[96,192]{1,0:T(8,128)}) %reduce-scatter.37.cloned.1.call-update) | async-done | bytes 73744 | tf_op jit(solution)/shard_map/reduce_scatter | solution.py:370
  1288.3 65.4 %reduce-scatter.33.cloned.1.call-done = f32[96,192]{1,0:T(8,128)} async-done(((f32[768,192]{1,0:T(8,128)}), f32[96,192]{1,0:T(8,128)}) %reduce-scatter.33.cloned.1.call-update) | async-done | bytes 73744 | tf_op jit(solution)/shard_map/reduce_scatter | solution.py:368
  1353.7 65.9 %reduce-scatter.35.cloned.1.call-done = f32[96,192]{1,0:T(8,128)} async-done(((f32[768,192]{1,0:T(8,128)}), f32[96,192]{1,0:T(8,128)}) %reduce-scatter.35.cloned.1.call-update) | async-done | bytes 73744 | tf_op jit(solution)/shard_map/reduce_scatter | solution.py:369
  1419.6 71.9 %reduce-scatter.39.cloned.1.call-done = f32[96,768]{1,0:T(8,128)} async-done(((f32[768,768]{1,0:T(8,128)}), f32[96,768]{1,0:T(8,128)}) %reduce-scatter.39.cloned.1.call-update) | async-done | bytes 294928 | tf_op jit(solution)/shard_map/reduce_scatter | solution.py:372
  1491.5 72.1 %reduce-scatter.41.cloned.1.call-done = f32[768,96]{0,1:T(8,128)} async-done(((f32[768,768]{0,1:T(8,128)}), f32[768,96]{0,1:T(8,128)}) %reduce-scatter.41.cloned.1.call-update) | async-done | bytes 294928 | tf_op jit(solution)/shard_map/reduce_scatter | solution.py:373
  (382 shorter events, 386.4 us)
Async XLA Ops:
  8.0 159.7 %copy-start.8 = (bf16[128,768]{1,0:T(8,128)(2,1)S(1)}, bf16[128,768]{1,0:T(8,128)(2,1)}, u32[]{:S(2)}) copy-start(bf16[128,768]{1,0:T(8,128)(2,1)} %param.17) | copy-start | bytes 589828
  8.0 194.1 %reduce-scatter.23.cloned.1.call-start = ((), (), s32[]{:S(2)}) async-start(), calls=%async_computation.16 | async-start | bytes 983040 | tf_op jit(solution)/shard_map/reduce_scatter | solution.py:39
  12.4 164.5 %copy-start.81 = (f32[128]{0:T(128)}, f32[128]{0:T(128)S(1)}, u32[]{:S(2)}) copy-start(f32[128]{0:T(128)S(1)} %broadcast_multiply_fusion.1) | copy-start | bytes 1540
  13.6 163.3 %copy-start.86 = (f32[128]{0:T(128)}, f32[128]{0:T(128)S(1)}, u32[]{:S(2)}) copy-start(f32[128]{0:T(128)S(1)} %fusion.102) | copy-start | bytes 1540
  39.9 137.0 %copy-start.70 = (f32[768]{0:T(1024)}, f32[768]{0:T(1024)S(1)}, u32[]{:S(2)}) copy-start(f32[768]{0:T(1024)S(1)} %convert_element_type.270) | copy-start | bytes 9220
  74.6 105.7 %copy-start.30 = (bf16[192,768]{0,1:T(8,128)(2,1)}, bf16[192,768]{0,1:T(8,128)(2,1)S(1)}, u32[]{:S(2)}) copy-start(bf16[192,768]{0,1:T(8,128)(2,1)S(1)} %all_gather.75) | copy-start | bytes 884740
  105.8 71.6 %copy-start.28 = (bf16[768,192]{1,0:T(8,128)(2,1)}, bf16[768,192]{1,0:T(8,128)(2,1)S(1)}, u32[]{:S(2)}) copy-start(bf16[768,192]{1,0:T(8,128)(2,1)S(1)} %all_gather.72) | copy-start | bytes 884740
  182.3 41.4 %all-gather.5.cloned.1.call-start = ((), (), s32[]{:S(2)}) async-start(), calls=%async_computation.17 | async-start | bytes 1327104 | tf_op jit(solution)/shard_map/all_gather | solution.py:75
  183.1 83.5 %all-gather.7.cloned.1.call-start = ((), (), s32[]{:S(2)}) async-start(), calls=%async_computation.18 | async-start | bytes 1327104 | tf_op jit(solution)/shard_map/all_gather | solution.py:76
  183.8 116.8 %reduce-scatter.25.cloned.1.call-start = ((), (), s32[]{:S(2)}) async-start(), calls=%async_computation.19 | async-start | bytes 983040 | tf_op jit(solution)/shard_map/reduce_scatter | solution.py:39
  269.6 117.9 %all-gather.9.cloned.1.call-start = ((), (), s32[]{:S(2)}) async-start(), calls=%async_computation.20 | async-start | bytes 10485760 | tf_op jit(solution)/shard_map/all_gather | solution.py:45
  331.3 198.1 %all-gather.11.cloned.1.call-start = ((), (), s32[]{:S(2)}) async-start(), calls=%async_computation.21 | async-start | bytes 10485760 | tf_op jit(solution)/shard_map/all_gather | solution.py:45
  470.9 242.9 %reduce-scatter.49.cloned.1.call-start = ((), (), s32[]{:S(2)}) async-start(), calls=%async_computation.33 | async-start | bytes 1310720
  688.8 138.0 %reduce-scatter.51.cloned.1.call-start = ((), (), s32[]{:S(2)}) async-start(), calls=%async_computation.34 | async-start | bytes 1310720
  801.7 69.6 %reduce-scatter.27.cloned.1.call-start = ((), (), s32[]{:S(2)}) async-start(), calls=%async_computation.22 | async-start | bytes 983040 | tf_op jit(solution)/shard_map/reduce_scatter | solution.py:39
  847.9 61.9 %reduce-scatter.29.cloned.1.call-start = ((), (), s32[]{:S(2)}) async-start(), calls=%async_computation.23 | async-start | bytes 983040 | tf_op jit(solution)/shard_map/reduce_scatter | solution.py:39
  886.0 170.1 %reduce-scatter.53.cloned.1.call-start = ((), (), s32[]{:S(2)}) async-start(), calls=%async_computation.35 | async-start | bytes 884736
  927.0 130.8 %reduce-scatter.31.cloned.1.call-start = ((), (), s32[]{:S(2)}) async-start(), calls=%async_computation.24 | async-start | bytes 983040 | tf_op jit(solution)/shard_map/reduce_scatter | solution.py:39
  935.8 170.6 %reduce-scatter.47.cloned.1.call-start = ((), (), s32[]{:S(2)}) async-start(), calls=%async_computation.32 | async-start | bytes 1990656 | tf_op jit(solution)/shard_map/reduce_scatter | solution.py:376
  988.6 168.8 %reduce-scatter.45.cloned.1.call-start = ((), (), s32[]{:S(2)}) async-start(), calls=%async_computation.31 | async-start | bytes 1990656 | tf_op jit(solution)/shard_map/reduce_scatter | solution.py:375
  1042.5 180.1 %reduce-scatter.43.cloned.1.call-start = ((), (), s32[]{:S(2)}) async-start(), calls=%async_computation.30 | async-start | bytes 884736 | tf_op jit(solution)/shard_map/reduce_scatter | solution.py:374
  1045.0 243.4 %reduce-scatter.37.cloned.1.call-start = ((), (), s32[]{:S(2)}) async-start(), calls=%async_computation.27 | async-start | bytes 884736 | tf_op jit(solution)/shard_map/reduce_scatter | solution.py:370
  1046.4 307.3 %reduce-scatter.33.cloned.1.call-start = ((), (), s32[]{:S(2)}) async-start(), calls=%async_computation.25 | async-start | bytes 884736 | tf_op jit(solution)/shard_map/reduce_scatter | solution.py:368
  1047.8 371.8 %reduce-scatter.35.cloned.1.call-start = ((), (), s32[]{:S(2)}) async-start(), calls=%async_computation.26 | async-start | bytes 884736 | tf_op jit(solution)/shard_map/reduce_scatter | solution.py:369
  1049.3 442.2 %reduce-scatter.39.cloned.1.call-start = ((), (), s32[]{:S(2)}) async-start(), calls=%async_computation.28 | async-start | bytes 2654208 | tf_op jit(solution)/shard_map/reduce_scatter | solution.py:372
  1051.6 512.0 %reduce-scatter.41.cloned.1.call-start = ((), (), s32[]{:S(2)}) async-start(), calls=%async_computation.29 | async-start | bytes 2654208 | tf_op jit(solution)/shard_map/reduce_scatter | solution.py:373
  1055.3 49.0 %copy-start.27 = (f32[128,768]{1,0:T(8,128)S(1)}, f32[128,768]{1,0:T(8,128)}, u32[]{:S(2)}) copy-start(f32[128,768]{1,0:T(8,128)} %param.32) | copy-start | bytes 1179652
  1055.3 49.0 %copy-start.37 = (bf16[128,768]{1,0:T(8,128)(2,1)S(1)}, bf16[128,768]{1,0:T(8,128)(2,1)}, u32[]{:S(2)}) copy-start(bf16[128,768]{1,0:T(8,128)(2,1)} %reduce-scatter.29.cloned.1.call-done) | copy-start | bytes 589828
  1055.3 49.0 %copy-start.49 = (bf16[128,768]{1,0:T(8,128)(2,1)S(1)}, bf16[128,768]{1,0:T(8,128)(2,1)}, u32[]{:S(2)}) copy-start(bf16[128,768]{1,0:T(8,128)(2,1)} %reduce-scatter.27.cloned.1.call-done) | copy-start | bytes 589828
  1055.3 49.0 %copy-start.85 = (f32[128]{0:T(128)S(1)}, f32[128]{0:T(128)}, u32[]{:S(2)}) copy-start(f32[128]{0:T(128)} %copy-done.83) | copy-start | bytes 1540
  1055.3 49.0 %copy-start.89 = (f32[128]{0:T(128)S(1)}, f32[128]{0:T(128)}, u32[]{:S(2)}) copy-start(f32[128]{0:T(128)} %copy-done.88) | copy-start | bytes 1540
  1055.4 49.0 %copy-start.91 = (f32[128]{0:T(128)S(1)}, f32[128]{0:T(128)}, u32[]{:S(2)}) copy-start(f32[128]{0:T(128)} %copy-done.90) | copy-start | bytes 1540
  (85 other events, 766.7 us)
Sparse Core Ops, SparseCore 0:
  182.4 19.6 reduce-scatter.22
  269.7 21.7 reduce-scatter.24
  331.4 56.0 all-gather.8
  471.1 58.2 all-gather.10
  688.9 24.8 reduce-scatter.48
  801.9 24.8 reduce-scatter.50
  848.0 23.2 reduce-scatter.26
  886.1 23.6 reduce-scatter.28
Sparse Core Ops, SparseCore 1:
  185.8 37.8 all-gather.4
  226.5 40.0 all-gather.6
  927.1 62.9 reduce-scatter.52
  992.8 22.2 reduce-scatter.30
  1019.1 67.2 reduce-scatter.46
  1090.9 66.5 reduce-scatter.44
  1161.1 61.4 reduce-scatter.42
  1226.7 61.5 reduce-scatter.36
  1292.1 61.6 reduce-scatter.32
  1358.0 61.6 reduce-scatter.34
  1423.5 67.9 reduce-scatter.38
  1495.6 68.0 reduce-scatter.40
where the time goes:
time: 1590 us; the launch traced here: 1570 us
  waiting for transfers between devices  665 us (42%)
  blocking collectives  330 us (21%)
  local copies, waits for them, and re-layouts  317 us (20%)
  matrix products  141 us (9%)
  other arithmetic  97.2 us (6%)
  between operations  20.3 us (1%)
    concatenate x4, local copies, waits for them, and re-layouts, grad_columns(): jnp.concatenate([shifted(padded, 26 - offset, vox) for offset in range(27...  104 us
    unnamed x217, local copies, waits for them, and re-layouts  82.9 us
    dot_general x2, matrix products, conv_forward(): jnp.dot(padded.reshape(-1, padded.shape[-1]), wide_kernel, preferred_elem...  73.9 us
    reduce_scatter x1, waiting for transfers between devices, shards(): lax.psum_scatter(wgrad_down, 'dp', scatter_dimension=1, tiled=True)  72.1 us
    reduce_scatter x1, waiting for transfers between devices, shards(): lax.psum_scatter(wgrad_up, 'dp', scatter_dimension=0, tiled=True)  71.9 us
    reduce_scatter x1, waiting for transfers between devices, shards(): lax.psum_scatter(wgrad_key, 'dp', scatter_dimension=0, tiled=True)  65.9 us
    reduce_scatter x1, waiting for transfers between devices, shards(): lax.psum_scatter(wgrad_value, 'dp', scatter_dimension=0, tiled=True)  65.7 us
    reduce_scatter x1, waiting for transfers between devices, shards(): lax.psum_scatter(wgrad_query, 'dp', scatter_dimension=0, tiled=True)  65.4 us
  transfers between devices with their start and end apart: 20, of which 16 were waited for; matrix products, arithmetic and copies ran while one was open for 9% of the time, Pallas kernels for 0%

commit v1 on v0

v1 whole, which is shorter than its diff:
```python
import jax
import jax.numpy as jnp
from jax import lax
from jax.sharding import PartitionSpec as P

HD = 64
GRID = 8
LOW = jnp.bfloat16


def ring_order(size):
    if size % 2:
        return list(range(size))
    return list(range(0, size, 2)) + list(range(size - 1, 0, -2))


def layer_norm(rows):
    middle = jnp.mean(rows, axis=-1, keepdims=True)
    centred = rows - middle
    spread = jnp.mean(centred * centred, axis=-1, keepdims=True)
    scale = lax.rsqrt(spread + 1e-06)
    return centred * scale, scale


def layer_norm_back(grad_normed, normed, scale):
    mean_grad = jnp.mean(grad_normed, axis=-1, keepdims=True)
    mean_dot = jnp.mean(grad_normed * normed, axis=-1, keepdims=True)
    return scale * (grad_normed - mean_grad - normed * mean_dot)


def gelu_exact(value):
    return jax.nn.gelu(value, approximate=False)


def norm_act(conv_out, vox_mask):
    live = jnp.sum(vox_mask, axis=1, keepdims=True) * conv_out.shape[2] * conv_out.shape[3]
    middle = jnp.sum(conv_out * vox_mask, axis=(1, 2, 3), keepdims=True) / live
    centred = (conv_out - middle) * vox_mask
    spread = jnp.sum(centred * centred, axis=(1, 2, 3), keepdims=True) / live
    normed = (conv_out - middle) * lax.rsqrt(spread + 1e-05)
    return gelu_exact(normed) * vox_mask


def contract_first(left, right):
    return lax.dot_general(
        left, right, (((0,), (0,)), ((), ())), preferred_element_type=jnp.float32
    )


def contract_last(left, right):
    return lax.dot_general(
        left, right, (((1,), (1,)), ((), ())), preferred_element_type=jnp.float32
    )


def dot(left, right):
    return jnp.dot(left, right, preferred_element_type=jnp.float32)


class Ring:
    def __init__(self, size):
        self.size = size
        self.order = ring_order(size)
        self.ahead = [(self.order[i], self.order[(i + 1) % size]) for i in range(size)]
        self.behind = [(b, a) for a, b in self.ahead]
        place = [0] * size
        for at, index in enumerate(self.order):
            place[index] = at
        self.spot = jnp.array(place, jnp.int32)[lax.axis_index("dp")]

    def index_at(self, distance):
        return jnp.array(self.order, jnp.int32)[(self.spot + distance) % self.size]

    def send(self, value, forward):
        return lax.ppermute(value, "dp", self.ahead if forward else self.behind)

    def gather(self, block):
        size = self.size
        rows = block.shape[0]
        pieces = [(0, 0, block)]
        one = two = block
        for step in range(1, (size - 1) // 2 + 1):
            one = self.send(one, True)
            two = self.send(two, False)
            pieces.append((-step, 0, one))
            pieces.append((step, 0, two))
        if size % 2 == 0:
            half = rows // 2
            pieces.append((-(size // 2), 0, self.send(one[:half], True)))
            pieces.append((size // 2, half, self.send(two[half:], False)))
        full = jnp.zeros((size,) + block.shape, block.dtype)
        for distance, start, piece in pieces:
            full = lax.dynamic_update_slice(
                full, piece[None], (self.index_at(distance), start, 0)
            )
        return full

    def scatter(self, terms):
        size = self.size
        rows = terms.shape[1]
        low = terms.astype(LOW)

        def term(distance):
            return lax.dynamic_index_in_dim(low, self.index_at(distance), 0, keepdims=False)

        own = lax.dynamic_index_in_dim(terms, self.index_at(0), 0, keepdims=False)
        one = two = None
        reach = (size - 1) // 2
        if size % 2 == 0:
            half = rows // 2
            far = term(size // 2)
            one = self.send(far[:half], True)
            two = self.send(far[half:], False)
            above, below = term(reach), term(-reach)
            if reach == 0:
                return own + jnp.concatenate([one, two]).astype(jnp.float32)
            one = jnp.concatenate([above[:half] + one, above[half:]])
            two = jnp.concatenate([below[:half], below[half:] + two])
        else:
            if reach == 0:
                return own
            one, two = term(reach), term(-reach)
        for step in range(reach, 0, -1):
            one = self.send(one, True)
            two = self.send(two, False)
            if step > 1:
                one = one + term(step - 1)
                two = two + term(-(step - 1))
        return own + one.astype(jnp.float32) + two.astype(jnp.float32)


class Quad:
    def __init__(self):
        me = lax.axis_index("tensor")
        self.core = me % 2
        self.chip = me // 2

    def over_core(self, value):
        return lax.ppermute(value, "tensor", [(i, i ^ 1) for i in range(4)])

    def over_chip(self, value):
        return lax.ppermute(value, "tensor", [(i, i ^ 2) for i in range(4)])

    def gather(self, block):
        far = self.over_chip(block)
        near = self.over_core(block)
        far_near = self.over_core(far)
        first = self.core == 0
        here = jnp.stack([jnp.where(first, block, near), jnp.where(first, near, block)])
        there = jnp.stack([jnp.where(first, far, far_near), jnp.where(first, far_near, far)])
        left = self.chip == 0
        return jnp.concatenate([jnp.where(left, here, there), jnp.where(left, there, here)])

    def halves(self, value):
        blocks = value.reshape(2, 2, value.shape[0] // 4, value.shape[1])
        first = self.core == 0
        mine = jnp.where(first, blocks[:, 0], blocks[:, 1])
        other = jnp.where(first, blocks[:, 1], blocks[:, 0])
        return mine, other

    def reduce_half(self, partial):
        mine, other = self.halves(partial)
        summed = (mine + self.over_core(other.astype(LOW)).astype(jnp.float32)).astype(LOW)
        return summed.astype(jnp.float32) + self.over_chip(summed).astype(jnp.float32)

    def reduce_own(self, partial):
        mine, other = self.halves(partial)
        summed = mine + self.over_core(other.astype(LOW)).astype(jnp.float32)
        keep, give = self.pick(summed), self.pick(summed[::-1])
        return keep + self.over_chip(give.astype(LOW)).astype(jnp.float32)

    def pick(self, half):
        return jnp.where(self.chip == 0, half[0], half[1])

    def join(self, half):
        other = self.over_core(half)
        first = self.core == 0
        blocks = jnp.stack([jnp.where(first, half, other), jnp.where(first, other, half)], axis=1)
        return blocks.reshape(4 * half.shape[1], half.shape[2])


def conv_same(field, taps):
    return lax.conv_general_dilated(
        field,
        taps,
        (1, 1, 1),
        "SAME",
        dimension_numbers=("NDHWC", "DHWIO", "NDHWC"),
        preferred_element_type=jnp.float32,
    )


def conv_weight_grad(field, grad_out):
    grads = lax.conv_general_dilated(
        field,
        grad_out,
        (1, 1, 1),
        ((1, 1),) * 3,
        dimension_numbers=("CDHWN", "IDHWO", "DHWNC"),
        preferred_element_type=jnp.float32,
    )
    return grads.reshape(27, grads.shape[3], grads.shape[4]).transpose(1, 0, 2)


def shards(
    tokens,
    crop_depth,
    w_query,
    w_key,
    w_value,
    w_out,
    w_up,
    w_down,
    w_tconv,
    w_conv1,
    w_conv2,
    ln1_gain,
    ln1_bias,
    ln2_gain,
    ln2_bias,
    cot_out,
    cot_dec,
    groups,
):
    ring = Ring(groups)
    quad = Quad()
    grid = GRID
    vox = 2 * grid
    patches = grid**3
    factor = HD ** (-0.5)
    width = w_query.shape[0] * groups
    part = w_query.shape[0]
    heads_here = w_query.shape[1] // HD
    span = heads_here * HD
    chans = w_conv1.shape[0] * groups
    chans_here = w_conv1.shape[2]

    low = lambda value: value.astype(LOW)
    rows_in = low(quad.gather(tokens).reshape(patches, width)).astype(jnp.float32)

    norm_params = jnp.stack([ln1_gain, ln1_bias, ln2_gain, ln2_bias])
    params = low(jnp.pad(norm_params, ((0, 12), (0, 4 * span - part))))
    pack_a = jnp.concatenate(
        [jnp.concatenate([low(w_query), low(w_key), low(w_value), low(w_out).T], axis=1), params]
    )
    pack_b = jnp.concatenate([low(w_up), low(w_down).T, low(w_tconv)], axis=1)
    pack_c = jnp.concatenate([low(w_conv1), low(w_conv2)], axis=2)
    pack_c = pack_c.reshape(pack_c.shape[0], -1)
    full_a = ring.gather(pack_a)
    full_b = ring.gather(pack_b).reshape(width, -1)
    full_c = ring.gather(pack_c).reshape(chans, 27, 2 * chans_here)

    norm_rows = full_a[:, part : part + 4, :part].astype(jnp.float32)
    gain_one, shift_one, gain_two, shift_two = norm_rows.transpose(1, 0, 2).reshape(4, width)
    matrix_a = full_a[:, :part].reshape(width, 4 * span)
    qkv_weight = matrix_a[:, : 3 * span]
    out_weight = matrix_a[:, 3 * span :]
    hidden_here = w_up.shape[1]
    up_weight = full_b[:, :hidden_here]
    down_weight = full_b[:, hidden_here : 2 * hidden_here]
    tconv_here = full_b[:, 2 * hidden_here :]
    out_full = quad.gather(out_weight).transpose(1, 0, 2).reshape(width, -1)
    tconv_full = quad.gather(tconv_here).transpose(1, 0, 2).reshape(width, -1)
    conv_full = quad.gather(full_c.reshape(chans, -1)).reshape(4, chans, 27, 2, chans_here)
    conv_full = conv_full.transpose(3, 1, 2, 0, 4).reshape(2, chans, 27, chans)
    taps_one = conv_full[0].transpose(1, 0, 2).reshape(3, 3, 3, chans, chans)
    taps_two = conv_full[1].transpose(1, 0, 2).reshape(3, 3, 3, chans, chans)
    back_one = taps_one[::-1, ::-1, ::-1].transpose(0, 1, 2, 4, 3)
    back_two = taps_two[::-1, ::-1, ::-1].transpose(0, 1, 2, 4, 3)

    key_live = jnp.arange(patches) // (grid * grid) < crop_depth[0]
    vox_mask = (jnp.arange(vox) < 2 * crop_depth[0]).astype(jnp.float32)[
        None, :, None, None, None
    ]

    cot_rows = quad.gather(cot_out).reshape(patches, width)
    cot_field = quad.gather(low(cot_dec).reshape(vox**3, chans_here)).transpose(1, 0, 2)
    cot_field = cot_field.reshape(1, vox, vox, vox, chans).astype(jnp.float32)

    normed_one, scale_one = layer_norm(rows_in)
    h_one = low(normed_one * gain_one + shift_one)
    qkv = low(dot(h_one, qkv_weight))

    def heads_view(flat):
        return flat.reshape(patches, heads_here, HD)

    query = heads_view(qkv[:, :span])
    keys = heads_view(qkv[:, span : 2 * span])
    values = heads_view(qkv[:, 2 * span :])
    scores = jnp.einsum("qhd,khd->hqk", query, keys, preferred_element_type=jnp.float32) * factor
    scores = jnp.where(key_live[None, None, :], scores, -1000000000.0)
    peak = jnp.max(scores, axis=-1, keepdims=True)
    expo = jnp.exp(scores - peak)
    probs = expo / jnp.sum(expo, axis=-1, keepdims=True)
    attended = jnp.einsum("hqk,khd->qhd", low(probs), values, preferred_element_type=jnp.float32)
    attended = low(attended.reshape(patches, span))
    attended_full = quad.gather(attended).transpose(1, 0, 2).reshape(patches, width)
    middle_rows = rows_in + contract_last(attended_full, out_full)
    normed_two, scale_two = layer_norm(middle_rows)
    h_two = low(normed_two * gain_two + shift_two)
    upper = dot(h_two, up_weight)
    hidden = low(gelu_exact(upper))
    mlp_half = quad.reduce_half(contract_last(hidden, down_weight))
    after_half = quad.halves(middle_rows)[0] + mlp_half
    after = quad.pick(after_half)
    dec_in = quad.join(low(after_half))

    tconv = dot(dec_in, tconv_full)
    cube = tconv.reshape(1, grid, grid, grid, chans, 2, 2, 2)
    cube = cube.transpose(0, 1, 5, 2, 6, 3, 7, 4).reshape(1, vox, vox, vox, chans)
    first = low(cube * vox_mask)
    conv_one = conv_same(first, taps_one)
    act_one, act_one_back = jax.vjp(lambda value: norm_act(value, vox_mask), conv_one)
    act_one = low(act_one)
    conv_two = conv_same(act_one, taps_two)
    act_two, act_two_back = jax.vjp(lambda value: norm_act(value, vox_mask), conv_two)

    def own_chans(field):
        return lax.dynamic_slice_in_dim(
            field, lax.axis_index("tensor") * chans_here, chans_here, axis=4
        )

    dec_out = own_chans(act_two)
    grad_conv_two = low(act_two_back(cot_field)[0])
    grad_act_one = conv_same(grad_conv_two, back_two)
    grad_conv_one = low(act_one_back(grad_act_one)[0])
    grad_first = conv_same(grad_conv_one, back_one)
    cube = (grad_first * vox_mask).reshape(grid, 2, grid, 2, grid, 2, chans)
    grad_tconv = low(cube.transpose(0, 2, 4, 6, 1, 3, 5).reshape(patches, 8 * chans))
    grad_after = cot_rows + contract_last(grad_tconv, tconv_full)
    grad_mlp = low(grad_after)

    grad_hidden = dot(grad_mlp, down_weight)
    grad_upper = low(jax.vjp(gelu_exact, upper)[1](grad_hidden)[0])
    grad_h_two = contract_last(grad_upper, up_weight)
    gain_two_terms = jnp.sum(grad_h_two * normed_two, axis=0)
    shift_two_terms = jnp.sum(grad_h_two, axis=0)
    norm_half = quad.reduce_half(grad_h_two)
    normed_half = quad.halves(normed_two)[0]
    scale_half = quad.halves(scale_two)[0]
    grad_mid_half = quad.halves(grad_after)[0] + layer_norm_back(
        norm_half * gain_two, normed_half, scale_half
    )
    grad_branch = quad.join(low(grad_mid_half))

    grad_attended = low(dot(grad_branch, out_weight))
    grad_heads = heads_view(grad_attended)
    low_probs = low(probs)
    grad_values = jnp.einsum("hqk,qhd->khd", low_probs, grad_heads, preferred_element_type=jnp.float32)
    grad_probs = jnp.einsum("qhd,khd->hqk", grad_heads, values, preferred_element_type=jnp.float32)
    inner = jnp.sum(probs * grad_probs, axis=-1, keepdims=True)
    grad_scores = low(probs * (grad_probs - inner))
    grad_query = factor * jnp.einsum(
        "hqk,khd->qhd", grad_scores, keys, preferred_element_type=jnp.float32
    )
    grad_keys = factor * jnp.einsum(
        "hqk,qhd->khd", grad_scores, query, preferred_element_type=jnp.float32
    )
    grad_qkv = jnp.concatenate(
        [low(grad.reshape(patches, span)) for grad in (grad_query, grad_keys, grad_values)], axis=1
    )
    grad_h_one = contract_last(grad_qkv, qkv_weight)
    gain_one_terms = jnp.sum(grad_h_one * normed_one, axis=0)
    shift_one_terms = jnp.sum(grad_h_one, axis=0)
    norm_own = quad.reduce_own(grad_h_one)
    normed_own = quad.pick(quad.halves(normed_one)[0])
    scale_own = quad.pick(quad.halves(scale_one)[0])
    grad_tokens = quad.pick(grad_mid_half) + layer_norm_back(
        norm_own * gain_one, normed_own, scale_own
    )

    def by_group(matrix):
        return matrix.reshape(groups, -1, matrix.shape[-1])

    conv_pack = jnp.concatenate(
        [
            conv_weight_grad(first, own_chans(grad_conv_one)),
            conv_weight_grad(act_one, own_chans(grad_conv_two)),
        ],
        axis=2,
    )
    conv_grads = ring.scatter(by_group(conv_pack.reshape(chans, -1)))
    conv_grads = conv_grads.reshape(-1, 27, 2 * chans_here)
    own_tconv = lax.dynamic_slice_in_dim(
        grad_tconv, lax.axis_index("tensor") * 8 * chans_here, 8 * chans_here, axis=1
    )
    mlp_pack = jnp.concatenate(
        [
            contract_first(h_two, grad_upper),
            contract_first(grad_mlp, hidden),
            contract_first(dec_in, own_tconv),
        ],
        axis=1,
    )
    mlp_grads = ring.scatter(by_group(mlp_pack))
    norm_terms = jnp.stack([gain_one_terms, shift_one_terms, gain_two_terms, shift_two_terms])
    norm_terms = lax.psum(norm_terms, "tensor")
    norm_terms = norm_terms.reshape(4, groups, part).transpose(1, 0, 2)
    norm_terms = jnp.pad(norm_terms, ((0, 0), (0, 12), (0, 4 * span - part)))
    attention_pack = jnp.concatenate(
        [contract_first(h_one, grad_qkv), contract_first(grad_branch, attended)], axis=1
    )
    attention_pack = jnp.concatenate([by_group(attention_pack), norm_terms], axis=1)
    attention_grads = ring.scatter(attention_pack)
    norm_grads = attention_grads[part : part + 4, :part]
    return (
        after,
        dec_out,
        grad_tokens,
        attention_grads[:part, :span],
        attention_grads[:part, span : 2 * span],
        attention_grads[:part, 2 * span : 3 * span],
        attention_grads[:part, 3 * span :].T,
        mlp_grads[:, :hidden_here],
        mlp_grads[:, hidden_here : 2 * hidden_here].T,
        mlp_grads[:, 2 * hidden_here :],
        conv_grads[:, :, :chans_here],
        conv_grads[:, :, chans_here:],
        norm_grads[0],
        norm_grads[1],
        norm_grads[2],
        norm_grads[3],
    )


def solution(mesh):
    in_specs = (
        P(("dp", "tensor"), None),
        P("dp"),
        P("dp", "tensor"),
        P("dp", "tensor"),
        P("dp", "tensor"),
        P("tensor", "dp"),
        P("dp", "tensor"),
        P("tensor", "dp"),
        P("dp", "tensor"),
        P("dp", None, "tensor"),
        P("dp", None, "tensor"),
        P("dp"),
        P("dp"),
        P("dp"),
        P("dp"),
        P(("dp", "tensor"), None),
        P("dp", None, None, None, "tensor"),
    )
    out_specs = (
        P(("dp", "tensor"), None),
        P("dp", None, None, None, "tensor"),
        P(("dp", "tensor"), None),
        P("dp", "tensor"),
        P("dp", "tensor"),
        P("dp", "tensor"),
        P("tensor", "dp"),
        P("dp", "tensor"),
        P("tensor", "dp"),
        P("dp", "tensor"),
        P("dp", None, "tensor"),
        P("dp", None, "tensor"),
        P("dp"),
        P("dp"),
        P("dp"),
        P("dp"),
    )
    groups = mesh.shape["dp"]

    def run(*arrays):
        return shards(*arrays, groups)

    return jax.shard_map(run, mesh=mesh, in_specs=in_specs, out_specs=out_specs, check_vma=False)
```

time: 1590 us -> 587 us (0.37)
  waiting for transfers between devices: 665 us -> 77.6 us
  blocking collectives: 330 us -> 10.2 us
  local copies, waits for them, and re-layouts: 317 us -> 178 us
  starting transfers between devices: 1.32 us -> 61 us
  matrix products: 141 us -> 121 us
    reduce_scatter x13 -> x0, waiting for transfers between devices: 523 us -> none  [the longest x1 72.1 us: shards(): lax.psum_scatter(wgrad_down, 'dp', scatter_dimension=1, tiled=True)]
    all_gather x12 -> x0, blocking collectives: 262 us -> none  [the longest x5 42.2 us: gather_rows(): return lax.all_gather(rows, 'tensor', axis=0, tiled=True)]
    all_gather x4 -> x0, waiting for transfers between devices: 92.6 us -> none  [the longest x2 46.5 us: gather_channels(): return lax.all_gather(field, 'tensor', axis=4, tiled=True)]
    concatenate x4, local copies, waits for them, and re-layouts: 104 us -> 11.9 us  [the longest x1 6.15 us: shards(): jnp.concatenate([contract_first(h_two, grad_upper), contract_first(grad_m...]
    dot_general x17 -> x10, matrix products: 101 us -> 15.4 us  [the longest x5 11 us: dot(): return jnp.dot(left, right, preferred_element_type=jnp.float32)]
    conv_general_dilated x0 -> x6, matrix products: none -> 83.2 us  [the longest x4 49.2 us: conv_same(): lax.conv_general_dilated(field, taps, (1, 1, 1), 'SAME', dimension_number...]
    ppermute x0 -> x77, waiting for transfers between devices: none -> 77.6 us  [the longest x48 56.1 us: send(): return lax.ppermute(value, 'dp', self.ahead if forward else self.behind)]
    unnamed x217 -> x160, local copies, waits for them, and re-layouts: 82.9 us -> 16.3 us
  transfers between devices with their start and end apart: 20 -> 77, of which waited for: 16 -> 32; matrix products, arithmetic and copies ran while one was open for 9% -> 28% of each run, Pallas kernels for 0% -> 0%
where the time goes in v1:
time: 587 us; the launch traced here: 576 us
  local copies, waits for them, and re-layouts  178 us (30%)
  matrix products  121 us (21%)
  other arithmetic  100 us (17%)
  waiting for transfers between devices  77.6 us (13%)
  starting transfers between devices  61 us (10%)
  between operations  29.1 us (5%)
  blocking collectives  10.2 us (2%)
    convert_element_type x11, local copies, waits for them, and re-layouts, shards(): low = lambda value: value.astype(LOW)  58 us
    ppermute x48, waiting for transfers between devices, send(): return lax.ppermute(value, 'dp', self.ahead if forward else self.behind)  56.1 us
    ppermute x48, starting transfers between devices, send(): return lax.ppermute(value, 'dp', self.ahead if forward else self.behind)  50.1 us
    conv_general_dilated x4, matrix products, conv_same(): lax.conv_general_dilated(field, taps, (1, 1, 1), 'SAME', dimension_number...  49.2 us
    conv_general_dilated x2, matrix products, conv_weight_grad(): lax.conv_general_dilated(field, grad_out, (1, 1, 1), ((1, 1),) * 3, dimen...  34 us
    convert_element_type x18, other arithmetic, shards(): low = lambda value: value.astype(LOW)  23.1 us
    dynamic_update_slice x25, local copies, waits for them, and re-layouts, gather(): lax.dynamic_update_slice(full, piece[None], (self.index_at(distance), sta...  20.9 us
    ppermute x10, waiting for transfers between devices, over_chip(): return lax.ppermute(value, 'tensor', [(i, i ^ 2) for i in range(4)])  19.9 us
  transfers between devices with their start and end apart: 77, of which 32 were waited for; matrix products, arithmetic and copies ran while one was open for 28% of the time, Pallas kernels for 0%

profile of v1, /device:TPU:0, one launch (start us, length us, event | category | flops | bytes accessed | tf_op | source)
XLA Modules:
  0.0 576.4 jit_solution(7922411961736418517)
XLA Ops:
  4.5 3.0 collective-permute-start.17
  68.9 3.6 collective-permute-done.34
  77.2 3.6 collective-permute-done.36
  131.0 4.7 collective-permute-done.8
  147.9 5.9 %copy.339 = f32[4096,4,32]{2,1,0:T(4,128)} copy(f32[4096,4,32]{0,2,1:T(8,128)S(1)} %convert_bitcast_fusion) | data formatting | bytes 4194304 | tf_op jit(solution)/shard_map/convert_element_type | solution.py:278
  153.8 7.7 %reshape.696 = f32[1,16,16,16,128]{4,3,2,1,0:T(8,128)} reshape(f32[4096,4,32]{2,1,0:T(4,128)} %copy.339) | data formatting | bytes 4194304 | tf_op jit(solution)/shard_map/convert_element_type | solution.py:278
  163.6 3.3 collective-permute-done.10
  191.2 4.4 collective-permute-done.21
  207.6 6.3 %multiply_convert_fusion.4 = (bf16[512,768]{1,0:T(8,128)(2,1)S(1)}, f32[512,768]{1,0:T(8,128)}, f32[512,768]{1,0:T(8,128)}) fusion(bf16[768,1792]{1,0:T(8,128)(2,1)} %bitcast.63, f32[512,768]{1,0:T(8,128)S(1)} %subtract_multiply_fusion, f32[768]{0:T(1024)S(1)} %add.610, f32[768]{0:T(1024)S(1)} %mul.438), kind=kOutput, calls=%fused_computation.125 | convolution fusion | flops 630718464 | bytes 6690816 | tf_op jit(solution)/shard_map/dot_general | solution.py:57
  223.0 8.9 %collective-permute-done.29 = bf16[768,256]{1,0:T(8,128)(2,1)S(1)} collective-permute-done((bf16[768,256]{1,0:T(8,128)(2,1)S(1)}, bf16[768,256]{1,0:T(8,128)(2,1)S(1)}, u32[]{:S(2)}, u32[]{:S(2)}) %collective-permute-start.29) | collective-permute-done | bytes 393248 | tf_op jit(solution)/shard_map/ppermute | solution.py:142
  233.0 7.0 %collective-permute-done.26 = bf16[2,128,768]{2,1,0:T(8,128)(2,1)S(1)} collective-permute-done((bf16[2,128,768]{2,1,0:T(8,128)(2,1)S(1)}, bf16[2,128,768]{2,1,0:T(8,128)(2,1)S(1)}, u32[]{:S(2)}, u32[]{:S(2)}) %collective-permute-start.26) | collective-permute-done | bytes 393248 | tf_op jit(solution)/shard_map/ppermute | solution.py:142
  256.7 12.0 %select_reduce_fusion.7 = (f32[128]{0:T(128)S(1)}, f32[16,16,8,3,128]{4,2,3,1,0:T(8,128)S(1)}) fusion(f32[16]{0:T(128)S(1)} %compare_convert_fusion, pred[8,3]{0,1:T(4,128)(4,1)S(1)} %copy-done.61, bf16[3,3,3,128,128]{3,4,2,1,0:T(8,128)(2,1)S(1)} %bitcast.675, bf16[16,16,1,7,2,128]{5,3,4,1,0,2:T(8,128)(2,1)S(1)} %slice.442, ...), kind=kOutput, calls=%fused_computation.48 | convolution fusion | flops 5003280384 | bytes 6521432 | tf_op jit(solution)/shard_map/conv_general_dilated | solution.py:183
  269.7 7.6 %fusion.49 = (bf16[16,16,8,3,128]{4,2,3,1,0:T(8,128)(2,1)S(1)}, f32[16,16,8,3,128]{4,2,3,1,0:T(8,128)S(1)}) fusion(f32[128]{0:T(128)S(1)} %get-tuple-element.111, f32[16]{0:T(128)S(1)} %compare_convert_fusion, pred[8,3]{0,1:T(4,128)(4,1)S(1)} %copy-done.61, f32[128]{0:T(128)S(1)} %broadcast_divide_fusion.2, f32[16,16,8,3,128]{4,2,3,1,0:T(8,128)S(1)} %get-tuple-element.240), kind=kLoop, calls=%fused_computation.100 | loop fusion | flops 55050240 | bytes 7865432 | tf_op jit(solution)/shard_map/convert_element_type | solution.py:238
  279.8 12.3 %select_reduce_fusion.4 = (f32[128]{0:T(128)S(1)}, f32[16,16,8,3,128]{4,2,3,1,0:T(8,128)S(1)}) fusion(f32[16]{0:T(128)S(1)} %compare_convert_fusion, pred[8,3]{0,1:T(4,128)(4,1)S(1)} %copy-done.61, bf16[3,3,3,128,128]{3,4,2,1,0:T(8,128)(2,1)S(1)} %bitcast.677, bf16[16,16,1,8,1,128]{5,3,4,1,0,2:T(8,128)(2,1)S(1)} %pad.14, ...), kind=kOutput, calls=%fused_computation.32 | convolution fusion | flops 5002493952 | bytes 6652504 | tf_op jit(solution)/shard_map/conv_general_dilated | solution.py:183
  293.6 7.8 %multiply_multiply_fusion = (f32[16,16,8,3,128]{4,2,3,1,0:T(8,128)}, f32[16,16,8,3,128]{4,2,3,1,0:T(8,128)S(1)}, f32[16,16,8,3,128]{4,2,3,1,0:T(8,128)S(1)}, f32[16,16,8,3,128]{4,2,3,1,0:T(8,128)S(1)}) fusion(f32[16]{0:T(128)S(1)} %compare_convert_fusion, f32[16,16,8,3,128]{4,2,3,1,0:T(8,128)S(1)} %get-tuple-element.108, f32[128]{0:T(128)S(1)} %get-tuple-element.105), kind=kLoop, calls=%fused_computation.17 | loop fusion | flops 51904512 | bytes 15729216 | tf_op jit(solution)/shard_map/jvp()/mul | solution.py:41
  307.5 10.0 %multiply_reduce_fusion.4 = (f32[128]{0:T(128)S(1)}, f32[128]{0:T(128)S(1)}, f32[1,16,16,16,128]{4,0,3,2,1:T(1,128)S(1)}) fusion(f32[128]{0:T(128)S(1)} %get-tuple-element.105, f32[1,16,16,16,128]{4,0,3,2,1:T(1,128)S(1)} %bitcast.640, f32[1,16,16,16,128]{4,0,3,2,1:T(1,128)S(1)} %bitcast.639, f32[1,16,16,16,128]{4,0,3,2,1:T(1,128)S(1)} %bitcast.638, ...), kind=kLoop, calls=%fused_computation.160 | loop fusion | flops 6815488 | bytes 12584512 | tf_op jit(solution)/shard_map/transpose(jvp())/reduce_sum | solution.py:40
  319.9 3.0 add_convert_fusion.1
  324.6 13.5 %select_reduce_fusion.1 = (f32[128]{0:T(128)S(1)}, f32[128]{0:T(128)S(1)}, f32[16,16,8,3,128]{4,2,3,1,0:T(8,128)S(1)}) fusion(f32[128]{0:T(128)S(1)} %get-tuple-element.111, pred[8,3]{0,1:T(4,128)(4,1)S(1)} %copy-done.61, f32[128]{0:T(128)S(1)} %broadcast_divide_fusion.2, f32[16,16,8,3,128]{4,2,3,1,0:T(8,128)S(1)} %get-tuple-element.240, ...), kind=kOutput, calls=%fused_computation.15 | convolution fusion | flops 5019009024 | bytes 12814424 | tf_op jit(solution)/shard_map/conv_general_dilated | solution.py:183
  340.7 4.1 constant_dynamic-slice_fusion.1
  346.6 27.5 %fusion.44 = f32[3,3,3,128,32]{3,4,2,1,0:T(8,128)} fusion(bf16[1,16,16,16,128]{4,0,3,2,1:T(2,128)(2,1)S(1)} %multiply_convert_fusion.3, bf16[1,16,16,16,128]{4,0,3,2,1:T(2,128)(2,1)S(1)} %add_convert_fusion, s32[]{:T(128)S(6)} %select_n.873), kind=kOutput, calls=%fused_computation.95 | convolution fusion | flops 797376512 | bytes 2539524 | tf_op jit(solution)/shard_map/conv_general_dilated | solution.py:194
  376.3 11.4 %multiply_convert_fusion = bf16[16,16,8,3,128]{4,2,3,1,0:T(8,128)(2,1)S(1)} fusion(f32[16]{0:T(128)S(1)} %compare_convert_fusion, pred[8,3]{0,1:T(4,128)(4,1)S(1)} %copy-done.61, bf16[3,3,3,128,128]{3,4,2,1,0:T(8,128)(2,1)S(1)} %bitcast.676, bf16[16,16,1,7,2,128]{5,3,4,1,0,2:T(8,128)(2,1)S(1)} %slice.457, bf16[16,16,1,8,3,128]{5,3,4,1,0,2:T(8,128)(2,1)S(1)} %copy.356), kind=kOutput, calls=%fused_computation.13 | convolution fusion | flops 5002493952 | bytes 4948056 | tf_op jit(solution)/shard_map/conv_general_dilated | solution.py:183
  389.2 27.9 %copy.358 = bf16[8,2,8,2,8,2,128]{4,2,0,5,3,1,6:T(8,128)(2,1)} copy(bf16[8,2,8,2,8,2,128]{6,3,2,5,4,1,0:T(2,128)(2,1)} %bitcast.654) | data formatting | bytes 2097152 | tf_op jit(solution)/shard_map/convert_element_type | solution.py:238
  417.1 25.2 %convert_element_type.304 = bf16[512,1024]{0,1:T(8,128)(2,1)} reshape(bf16[8,8,8,128,2,2,2]{2,1,0,6,5,4,3:T(8,128)(2,1)} %bitcast.612) | data formatting | bytes 2097152 | tf_op jit(solution)/shard_map/convert_element_type | solution.py:238
  442.2 3.3 bitcast_add_fusion
  453.6 3.4 multiply_reduce_fusion.2
  460.1 6.5 %fusion.4 = f32[3,3,3,128,32,1]{3,4,2,5,1,0:T(8,128)S(1)} fusion(bf16[16,16,8,3,32,1]{4,1,3,2,0,5:T(8,128)(2,1)S(1)} %bitcast.673, bf16[16,16,8,3,128,1]{4,2,3,1,0,5:T(8,128)(2,1)S(1)} %maximum_bitcast_fusion.5, bf16[16,16,8,3,128,1]{4,2,3,1,0,5:T(8,128)(2,1)S(1)} %bitcast.623, bf16[16,16,8,3,128,1]{4,2,3,1,0,5:T(8,128)(2,1)S(1)} %maximum_bitcast_fusion.4), kind=kOutput, calls=%fused_computation.9 | convolution fusion | flops 1252786176 | bytes 5554176 | tf_op jit(solution)/shard_map/conv_general_dilated | solution.py:194
  466.7 3.0 copy.383
  475.4 4.4 pad_maximum_fusion
  479.8 6.1 %copy.379 = f32[768,1792]{1,0:T(8,128)} copy(f32[768,1792]{0,1:T(8,128)} %pad_maximum_fusion) | data formatting | bytes 11010048 | tf_op jit(solution)/shard_map/concatenate | solution.py:387
  486.0 3.0 convert_element_type.336
  538.4 10.2 %psum.7 = f32[8,4,96]{2,1,0:T(4,128)S(1)} all-reduce(f32[8,4,96]{2,1,0:T(4,128)S(1)} %bitcast.694), channel_id=1, replica_groups=mesh['dp'=8,'tensor'=4] {'tensor'}, use_global_device_ids=true, to_apply=%region_26.27 | all-reduce | flops 3072 | bytes 24576 | tf_op jit(solution)/shard_map/psum | solution.py:397
  557.1 3.1 collective-permute-done.58
  (562 shorter events, 283.6 us)
Async XLA Ops:
  4.5 101.8 %collective-permute-start.17 = (bf16[96,1792]{1,0:T(8,128)(2,1)}, bf16[96,1792]{1,0:T(8,128)(2,1)}, u32[]{:S(2)}, u32[]{:S(2)}) collective-permute-start(bf16[96,1792]{1,0:T(8,128)(2,1)} %pad_maximum_fusion.23), channel_id=1, source_target_pairs={{0,8},{8,16},{16,24},{24,28},{28,20},{20,12},{12,4},{4,0},{1,9},{9... | collective-permute-start | bytes 1032200 | tf_op jit(solution)/shard_map/ppermute | solution.py:75
  7.5 102.2 %collective-permute-start.18 = (bf16[96,1792]{1,0:T(8,128)(2,1)}, bf16[96,1792]{1,0:T(8,128)(2,1)}, u32[]{:S(2)}, u32[]{:S(2)}) collective-permute-start(bf16[96,1792]{1,0:T(8,128)(2,1)} %pad_maximum_fusion.23), channel_id=1, source_target_pairs={{8,0},{16,8},{24,16},{28,24},{20,28},{12,20},{4,12},{0,4},{9,1},{1... | collective-permute-start | bytes 1032200 | tf_op jit(solution)/shard_map/ppermute | solution.py:75
  25.5 57.4 %collective-permute-start.3 = (bf16[112,768]{1,0:T(8,128)(2,1)}, bf16[112,768]{1,0:T(8,128)(2,1)}, u32[]{:S(2)}, u32[]{:S(2)}) collective-permute-start(bf16[112,768]{1,0:T(8,128)(2,1)} %get-tuple-element.118), channel_id=1, source_target_pairs={{0,8},{8,16},{16,24},{24,28},{28,20},{20,12},{12,4},{4,0},{1,9},{9... | collective-permute-start | bytes 516104 | tf_op jit(solution)/shard_map/ppermute | solution.py:75
  27.6 56.4 %collective-permute-start.4 = (bf16[112,768]{1,0:T(8,128)(2,1)}, bf16[112,768]{1,0:T(8,128)(2,1)}, u32[]{:S(2)}, u32[]{:S(2)}) collective-permute-start(bf16[112,768]{1,0:T(8,128)(2,1)} %get-tuple-element.118), channel_id=1, source_target_pairs={{8,0},{16,8},{24,16},{28,24},{20,28},{12,20},{4,12},{0,4},{9,1},{1... | collective-permute-start | bytes 516104 | tf_op jit(solution)/shard_map/ppermute | solution.py:75
  30.1 29.5 %collective-permute-start.31 = (bf16[16,1728]{1,0:T(8,128)(2,1)}, bf16[16,1728]{1,0:T(8,128)(2,1)}, u32[]{:S(2)}, u32[]{:S(2)}) collective-permute-start(bf16[16,1728]{1,0:T(8,128)(2,1)} %reshape.623), channel_id=1, source_target_pairs={{0,8},{8,16},{16,24},{24,28},{28,20},{20,12},{12,4},{4,0},{1,9},{9... | collective-permute-start | bytes 165896 | tf_op jit(solution)/shard_map/ppermute | solution.py:75
  80.8 32.6 %collective-permute-start.1 = (bf16[128,768]{1,0:T(8,128)(2,1)}, bf16[128,768]{1,0:T(8,128)(2,1)}, u32[]{:S(2)}, u32[]{:S(2)}) collective-permute-start(bf16[128,768]{1,0:T(8,128)(2,1)} %param.69), channel_id=1, source_target_pairs={{0,2},{1,3},{2,0},{3,1},{4,6},{5,7},{6,4},{7,5},{8,10},{9,11},{10,... | collective-permute-start | bytes 589832 | tf_op jit(solution)/shard_map/ppermute | solution.py:142
  92.3 12.6 %collective-permute-start.46 = (bf16[4096,32]{0,1:T(8,128)(2,1)}, bf16[4096,32]{0,1:T(8,128)(2,1)}, u32[]{:S(2)}, u32[]{:S(2)}) collective-permute-start(bf16[4096,32]{0,1:T(8,128)(2,1)} %copy.327), channel_id=1, source_target_pairs={{0,2},{1,3},{2,0},{3,1},{4,6},{5,7},{6,4},{7,5},{8,10},{9,11},{10,... | collective-permute-start | bytes 786440 | tf_op jit(solution)/shard_map/ppermute | solution.py:142
  94.6 68.3 %collective-permute-start.43 = (f32[128,768]{1,0:T(8,128)}, f32[128,768]{1,0:T(8,128)}, u32[]{:S(2)}, u32[]{:S(2)}) collective-permute-start(f32[128,768]{1,0:T(8,128)} %param.84), channel_id=1, source_target_pairs={{0,2},{1,3},{2,0},{3,1},{4,6},{5,7},{6,4},{7,5},{8,10},{9,11},{10,... | collective-permute-start | bytes 1179656 | tf_op jit(solution)/shard_map/ppermute | solution.py:142
  104.9 18.3 %collective-permute-start.42 = (f32[128,768]{1,0:T(8,128)}, f32[128,768]{1,0:T(8,128)}, u32[]{:S(2)}, u32[]{:S(2)}) collective-permute-start(f32[128,768]{1,0:T(8,128)} %param.84), channel_id=1, source_target_pairs={{0,1},{1,0},{2,3},{3,2},{4,5},{5,4},{6,7},{7,6},{8,9},{9,8},{10,11... | collective-permute-start | bytes 1179656 | tf_op jit(solution)/shard_map/ppermute | solution.py:139
  113.4 60.9 %collective-permute-start.39 = (bf16[128,1728]{1,0:T(8,128)(2,1)}, bf16[128,1728]{1,0:T(8,128)(2,1)}, u32[]{:S(2)}, u32[]{:S(2)}) collective-permute-start(bf16[128,1728]{1,0:T(8,128)(2,1)} %bitcast.95), channel_id=1, source_target_pairs={{0,1},{1,0},{2,3},{3,2},{4,5},{5,4},{6,7},{7,6},{8,9},{9,8},{10,11... | collective-permute-start | bytes 1327112 | tf_op jit(solution)/shard_map/ppermute | solution.py:139
  113.4 67.4 %collective-permute-start.40 = (bf16[128,1728]{1,0:T(8,128)(2,1)}, bf16[128,1728]{1,0:T(8,128)(2,1)}, u32[]{:S(2)}, u32[]{:S(2)}) collective-permute-start(bf16[128,1728]{1,0:T(8,128)(2,1)} %bitcast.95), channel_id=1, source_target_pairs={{0,2},{1,3},{2,0},{3,1},{4,6},{5,7},{6,4},{7,5},{8,10},{9,11},{10,... | collective-permute-start | bytes 1327112 | tf_op jit(solution)/shard_map/ppermute | solution.py:142
  118.1 19.9 %collective-permute-start.47 = (bf16[4096,32]{0,1:T(8,128)(2,1)}, bf16[4096,32]{0,1:T(8,128)(2,1)}, u32[]{:S(2)}, u32[]{:S(2)}) collective-permute-start(bf16[4096,32]{0,1:T(8,128)(2,1)} %collective-permute-done.46), channel_id=1, source_target_pairs={{0,1},{1,0},{2,3},{3,2},{4,5},{5,4},{6,7},{7,6},{8,9},{9,8},{10,11... | collective-permute-start | bytes 786440 | tf_op jit(solution)/shard_map/ppermute | solution.py:139
  135.7 41.0 %collective-permute-start.19 = (bf16[96,1792]{1,0:T(8,128)(2,1)}, bf16[96,1792]{1,0:T(8,128)(2,1)}, u32[]{:S(2)}, u32[]{:S(2)}) collective-permute-start(bf16[96,1792]{1,0:T(8,128)(2,1)} %collective-permute-done.17), channel_id=1, source_target_pairs={{0,8},{8,16},{16,24},{24,28},{28,20},{20,12},{12,4},{4,0},{1,9},{9... | collective-permute-start | bytes 1032200 | tf_op jit(solution)/shard_map/ppermute | solution.py:75
  137.9 23.6 %collective-permute-start.9 = (bf16[56,768]{1,0:T(8,128)(2,1)}, bf16[56,768]{1,0:T(8,128)(2,1)}, u32[]{:S(2)}, u32[]{:S(2)}) collective-permute-start(bf16[56,768]{1,0:T(8,128)(2,1)} %slice.422), channel_id=1, source_target_pairs={{0,8},{8,16},{16,24},{24,28},{28,20},{20,12},{12,4},{4,0},{1,9},{9... | collective-permute-start | bytes 258056 | tf_op jit(solution)/shard_map/ppermute | solution.py:75
  162.9 16.1 %collective-permute-start.20 = (bf16[96,1792]{1,0:T(8,128)(2,1)}, bf16[96,1792]{1,0:T(8,128)(2,1)}, u32[]{:S(2)}, u32[]{:S(2)}) collective-permute-start(bf16[96,1792]{1,0:T(8,128)(2,1)} %collective-permute-done.18), channel_id=1, source_target_pairs={{8,0},{16,8},{24,16},{28,24},{20,28},{12,20},{4,12},{0,4},{9,1},{1... | collective-permute-start | bytes 1032200 | tf_op jit(solution)/shard_map/ppermute | solution.py:75
  167.0 15.3 %collective-permute-start.44 = (f32[128,768]{1,0:T(8,128)}, f32[128,768]{1,0:T(8,128)}, u32[]{:S(2)}, u32[]{:S(2)}) collective-permute-start(f32[128,768]{1,0:T(8,128)} %collective-permute-done.43), channel_id=1, source_target_pairs={{0,1},{1,0},{2,3},{3,2},{4,5},{5,4},{6,7},{7,6},{8,9},{9,8},{10,11... | collective-permute-start | bytes 1179656 | tf_op jit(solution)/shard_map/ppermute | solution.py:139
  174.3 10.8 %collective-permute-start.11 = (bf16[512,192]{0,1:T(8,128)(2,1)}, bf16[512,192]{0,1:T(8,128)(2,1)S(1)}, u32[]{:S(2)}, u32[]{:S(2)}) collective-permute-start(bf16[512,192]{0,1:T(8,128)(2,1)} %bitcast.38), channel_id=1, source_target_pairs={{0,1},{1,0},{2,3},{3,2},{4,5},{5,4},{6,7},{7,6},{8,9},{9,8},{10,11... | collective-permute-start | bytes 589832 | tf_op jit(solution)/shard_map/ppermute | solution.py:139
  182.3 18.3 %collective-permute-start.41 = (bf16[128,1728]{1,0:T(8,128)(2,1)}, bf16[128,1728]{1,0:T(8,128)(2,1)S(1)}, u32[]{:S(2)}, u32[]{:S(2)}) collective-permute-start(bf16[128,1728]{1,0:T(8,128)(2,1)} %collective-permute-done.40), channel_id=1, source_target_pairs={{0,1},{1,0},{2,3},{3,2},{4,5},{5,4},{6,7},{7,6},{8,9},{9,8},{10,11... | collective-permute-start | bytes 1327112 | tf_op jit(solution)/shard_map/ppermute | solution.py:139
  185.1 10.5 %collective-permute-start.21 = (bf16[96,1792]{1,0:T(8,128)(2,1)}, bf16[96,1792]{1,0:T(8,128)(2,1)S(1)}, u32[]{:S(2)}, u32[]{:S(2)}) collective-permute-start(bf16[96,1792]{1,0:T(8,128)(2,1)} %collective-permute-done.19), channel_id=1, source_target_pairs={{0,8},{8,16},{16,24},{24,28},{28,20},{20,12},{12,4},{4,0},{1,9},{9... | collective-permute-start | bytes 1032200 | tf_op jit(solution)/shard_map/ppermute | solution.py:75
  186.5 10.2 %collective-permute-start.22 = (bf16[96,1792]{1,0:T(8,128)(2,1)}, bf16[96,1792]{1,0:T(8,128)(2,1)S(1)}, u32[]{:S(2)}, u32[]{:S(2)}) collective-permute-start(bf16[96,1792]{1,0:T(8,128)(2,1)} %collective-permute-done.20), channel_id=1, source_target_pairs={{8,0},{16,8},{24,16},{28,24},{20,28},{12,20},{4,12},{0,4},{9,1},{1... | collective-permute-start | bytes 1032200 | tf_op jit(solution)/shard_map/ppermute | solution.py:75
  190.3 12.1 %collective-permute-start.16 = (bf16[768,192]{0,1:T(8,128)(2,1)}, bf16[768,192]{0,1:T(8,128)(2,1)}, u32[]{:S(2)}, u32[]{:S(2)}) collective-permute-start(bf16[768,192]{0,1:T(8,128)(2,1)} %collective-permute-done.15), channel_id=1, source_target_pairs={{0,1},{1,0},{2,3},{3,2},{4,5},{5,4},{6,7},{7,6},{8,9},{9,8},{10,11... | collective-permute-start | bytes 884744 | tf_op jit(solution)/shard_map/ppermute | solution.py:139
  219.9 12.0 %collective-permute-start.29 = (bf16[768,256]{1,0:T(8,128)(2,1)S(1)}, bf16[768,256]{1,0:T(8,128)(2,1)S(1)}, u32[]{:S(2)}, u32[]{:S(2)}) collective-permute-start(bf16[768,256]{1,0:T(8,128)(2,1)S(1)} %slice.441), channel_id=1, source_target_pairs={{0,2},{1,3},{2,0},{3,1},{4,6},{5,7},{6,4},{7,5},{8,10},{9,11},{10,... | collective-permute-start | bytes 1179656 | tf_op jit(solution)/shard_map/ppermute | solution.py:142
  220.5 11.4 %collective-permute-start.28 = (bf16[768,256]{1,0:T(8,128)(2,1)S(1)}, bf16[768,256]{1,0:T(8,128)(2,1)S(1)}, u32[]{:S(2)}, u32[]{:S(2)}) collective-permute-start(bf16[768,256]{1,0:T(8,128)(2,1)S(1)} %slice.441), channel_id=1, source_target_pairs={{0,1},{1,0},{2,3},{3,2},{4,5},{5,4},{6,7},{7,6},{8,9},{9,8},{10,11... | collective-permute-start | bytes 1179656 | tf_op jit(solution)/shard_map/ppermute | solution.py:139
  220.9 19.1 %collective-permute-start.26 = (bf16[2,128,768]{2,1,0:T(8,128)(2,1)S(1)}, bf16[2,128,768]{2,1,0:T(8,128)(2,1)S(1)}, u32[]{:S(2)}, u32[]{:S(2)}) collective-permute-start(bf16[2,128,768]{2,1,0:T(8,128)(2,1)S(1)} %fusion.102), channel_id=1, source_target_pairs={{0,2},{1,3},{2,0},{3,1},{4,6},{5,7},{6,4},{7,5},{8,10},{9,11},{10,... | collective-permute-start | bytes 1179656 | tf_op jit(solution)/shard_map/ppermute | solution.py:142
  472.0 19.2 %collective-permute-start.69 = (bf16[8,1728]{1,0:T(8,128)(2,1)S(1)}, bf16[8,1728]{1,0:T(8,128)(2,1)S(1)}, u32[]{:S(2)}, u32[]{:S(2)}) collective-permute-start(bf16[8,1728]{1,0:T(8,128)(2,1)S(1)} %get-tuple-element.199), channel_id=1, source_target_pairs={{0,8},{8,16},{16,24},{24,28},{28,20},{20,12},{12,4},{4,0},{1,9},{9... | collective-permute-start | bytes 82952 | tf_op jit(solution)/shard_map/ppermute | solution.py:75
  472.4 18.7 %collective-permute-start.73 = (bf16[8,1728]{1,0:T(8,128)(2,1)S(1)}, bf16[8,1728]{1,0:T(8,128)(2,1)S(1)}, u32[]{:S(2)}, u32[]{:S(2)}) collective-permute-start(bf16[8,1728]{1,0:T(8,128)(2,1)S(1)} %get-tuple-element.201), channel_id=1, source_target_pairs={{8,0},{16,8},{24,16},{28,24},{20,28},{12,20},{4,12},{0,4},{9,1},{1... | collective-permute-start | bytes 82952 | tf_op jit(solution)/shard_map/ppermute | solution.py:75
  489.1 14.8 %collective-permute-start.61 = (bf16[48,1792]{1,0:T(8,128)(2,1)S(1)}, bf16[48,1792]{1,0:T(8,128)(2,1)S(1)}, u32[]{:S(2)}, u32[]{:S(2)}) collective-permute-start(bf16[48,1792]{1,0:T(8,128)(2,1)S(1)} %get-tuple-element.130), channel_id=1, source_target_pairs={{0,8},{8,16},{16,24},{24,28},{28,20},{20,12},{12,4},{4,0},{1,9},{9... | collective-permute-start | bytes 516104 | tf_op jit(solution)/shard_map/ppermute | solution.py:75
  489.5 14.4 %collective-permute-start.65 = (bf16[48,1792]{1,0:T(8,128)(2,1)S(1)}, bf16[48,1792]{1,0:T(8,128)(2,1)S(1)}, u32[]{:S(2)}, u32[]{:S(2)}) collective-permute-start(bf16[48,1792]{1,0:T(8,128)(2,1)S(1)} %get-tuple-element.132), channel_id=1, source_target_pairs={{8,0},{16,8},{24,16},{28,24},{20,28},{12,20},{4,12},{0,4},{9,1},{1... | collective-permute-start | bytes 516104 | tf_op jit(solution)/shard_map/ppermute | solution.py:75
  494.2 16.2 %collective-permute-start.48 = (bf16[2,128,768]{2,1,0:T(8,128)(2,1)}, bf16[2,128,768]{2,1,0:T(8,128)(2,1)}, u32[]{:S(2)}, u32[]{:S(2)}) collective-permute-start(bf16[2,128,768]{2,1,0:T(8,128)(2,1)} %fusion.110), channel_id=1, source_target_pairs={{0,1},{1,0},{2,3},{3,2},{4,5},{5,4},{6,7},{7,6},{8,9},{9,8},{10,11... | collective-permute-start | bytes 1179656 | tf_op jit(solution)/shard_map/ppermute | solution.py:139
  524.4 26.9 %collective-permute-start.64 = (bf16[96,1792]{1,0:T(8,128)(2,1)}, bf16[96,1792]{1,0:T(8,128)(2,1)}, u32[]{:S(2)}, u32[]{:S(2)}) collective-permute-start(bf16[96,1792]{1,0:T(8,128)(2,1)} %get-tuple-element.124), channel_id=1, source_target_pairs={{0,8},{8,16},{16,24},{24,28},{28,20},{20,12},{12,4},{4,0},{1,9},{9... | collective-permute-start | bytes 1032200 | tf_op jit(solution)/shard_map/ppermute | solution.py:75
  525.1 26.2 %collective-permute-start.68 = (bf16[96,1792]{1,0:T(8,128)(2,1)S(1)}, bf16[96,1792]{1,0:T(8,128)(2,1)}, u32[]{:S(2)}, u32[]{:S(2)}) collective-permute-start(bf16[96,1792]{1,0:T(8,128)(2,1)S(1)} %get-tuple-element.125), channel_id=1, source_target_pairs={{8,0},{16,8},{24,16},{28,24},{20,28},{12,20},{4,12},{0,4},{9,1},{1... | collective-permute-start | bytes 1032200 | tf_op jit(solution)/shard_map/ppermute | solution.py:75
  551.0 12.6 %collective-permute-start.51 = (bf16[2,128,768]{2,1,0:T(8,128)(2,1)S(1)}, bf16[2,128,768]{2,1,0:T(8,128)(2,1)S(1)}, u32[]{:S(2)}, u32[]{:S(2)}) collective-permute-start(bf16[2,128,768]{2,1,0:T(8,128)(2,1)S(1)} %fusion.111), channel_id=1, source_target_pairs={{0,1},{1,0},{2,3},{3,2},{4,5},{5,4},{6,7},{7,6},{8,9},{9,8},{10,11... | collective-permute-start | bytes 1179656 | tf_op jit(solution)/shard_map/ppermute | solution.py:139
  (117 other events, 828.8 us)
